TPU v7x, 32 devices: a whole 2x2x4 slice. The times are simulated.
32 devices in a mesh: dp: 4 (over y, x), expert: 8 (over z, core).
Axes of the slice: x: 2, y: 2, z: 4, core: 2. Of those that a mesh axis runs over, the one named last changes fastest.
Arguments:
- tokens: bfloat16 [512, 1024], P(('dp', 'expert')), may hold values from -6 to 6
- upstream: bfloat16 [512, 1024], P(('dp', 'expert')), may hold values from -6 to 6
- expert_ids: int32 [512, 8], P(('dp', 'expert')), may hold values from 0 to 7, all different within a row; in each aligned block of 16 rows (0 to 15, 16 to 31, ...) at most 16 rows name the same one
- gates: float32 [512, 8], P(('dp', 'expert')), may hold values from 0.05 to 1
- relocate: int32 [8, 1], replicated, may hold values from 0 to 1, as said below
- w_gate_up: bfloat16 [8, 4, 384, 1024], P('expert', 'dp'), may hold values from -0.1875 to 0.1875
- w_down: bfloat16 [8, 4, 192, 1024], P('expert', 'dp'), may hold values from -0.21875 to 0.21875
Outputs:
- grad_tokens: bfloat16 [512, 1024], P(('dp', 'expert'))
- grad_gate_up: bfloat16 [8, 4, 384, 1024], P('expert', 'dp')
- grad_down: bfloat16 [8, 4, 192, 1024], P('expert', 'dp')
Inputs may be any that keep to these rules, and one draw needn't show every extreme that they name: `expert_ids`: each row names 8 different experts; the rows of one device name one expert at most 16 times, and some device reaches 16. `relocate`: the first and the second half of the rows are equal; both values occur.
All inputs are finite; a program needn't handle non-finite values.
Results may differ from a plain program's by a relative error of at most 0.0064.
Values may be sent and summed in bfloat16 or wider, within the bound.
No kernel may reach another device: no remote copies, remote signals or barrier semaphores. Data moves between devices by JAX's collectives and lax.ppermute only.
A program may use at most 64 MiB of HBM per device.

v0:
```python
import jax
import jax.numpy as jnp
from jax import lax
from jax.sharding import PartitionSpec as P

SLICES = 4


contract_last = (((1,), (1,)), ((), ()))
contract_first = (((0,), (0,)), ((), ()))


def swapped(block, axis, apart):
    count = lax.axis_size(axis)
    route = []
    for low in range(count):
        high = low | 1 << apart
        if high != low and high < count:
            route += [(low, high), (high, low)]
    return lax.ppermute(block, axis, route)


def silu_parts(values_in):
    sigmoid_of = jax.nn.sigmoid(values_in)
    return (values_in * sigmoid_of, sigmoid_of * (1.0 + values_in * (1.0 - sigmoid_of)))


def pick_entry(lookup_table, row_index, col_index):
    rows_hit = jnp.arange(lookup_table.shape[0], dtype=jnp.int32)[:, None] == row_index
    cols_hit = jnp.arange(lookup_table.shape[1], dtype=jnp.int32)[None, :] == col_index
    return jnp.sum(jnp.where(rows_hit & cols_hit, lookup_table, 0))


def per_device(tokens, upstream, expert_ids, gates, relocate, w_gate_up, w_down):
    n_rows = lax.axis_size("dp")
    n_cols = lax.axis_size("expert")
    slot_count = n_rows // SLICES
    experts = slot_count * n_cols
    tok_dev, feature_width = tokens.shape
    top_count = expert_ids.shape[1]
    capacity = min(tok_dev, max(2, (3 * tok_dev * top_count + 2 * experts - 1) // (2 * experts)))
    pair_count = tok_dev * top_count
    buffer_rows = experts * capacity
    slice_width = w_down.shape[2]
    col_block = n_cols // SLICES
    col_here = lax.axis_index("expert")
    row_here = lax.axis_index("dp")
    slot_here = row_here // SLICES
    slice_here = row_here % SLICES
    far_bit = n_cols.bit_length() - 2
    half_cols = n_cols // 2
    flat_ids = expert_ids.reshape(pair_count)
    home_column = flat_ids // slot_count
    slot_of = flat_ids % slot_count
    expert_iota = jnp.arange(experts, dtype=jnp.int32)
    relocated = jnp.sum(
        jnp.where(flat_ids[:, None] == expert_iota[None, :], relocate.reshape(experts)[None, :], 0),
        axis=1,
    )
    column = (home_column + half_cols * relocated) % n_cols
    pair_iota = jnp.arange(pair_count, dtype=jnp.int32)
    earlier = (flat_ids[:, None] == flat_ids[None, :]) & (pair_iota[None, :] < pair_iota[:, None])
    slot_rank = jnp.sum(earlier.astype(jnp.int32), axis=1)
    target = (slot_of * n_cols + column) * capacity + slot_rank
    placing = (target[None, :] == jnp.arange(buffer_rows, dtype=jnp.int32)[:, None]).astype(
        jnp.bfloat16
    )
    x_pairs = jnp.repeat(tokens, top_count, axis=0)
    d_pairs = (
        gates.reshape(pair_count, 1) * jnp.repeat(upstream, top_count, axis=0).astype(jnp.float32)
    ).astype(jnp.bfloat16)
    pair_data = jnp.stack([x_pairs, d_pairs])
    sent = jnp.einsum("bp,kpw->kbw", placing, pair_data, preferred_element_type=jnp.float32).astype(
        jnp.bfloat16
    )
    sent = sent.reshape(2, slot_count, n_cols, capacity, feature_width)
    at_column = lax.all_to_all(sent, "expert", split_axis=2, concat_axis=2, tiled=True)
    swapped_here = pick_entry(relocate, col_here, slot_here)
    own_pack = jnp.concatenate([w_gate_up, w_down], axis=2)
    far_pack = swapped(own_pack, "expert", far_bit)
    own_pack = jnp.where(swapped_here == 1, far_pack, own_pack)
    gate_up = own_pack[0, 0, : 2 * slice_width]
    down_rows = own_pack[0, 0, 2 * slice_width :]
    grouped = at_column.reshape(2, n_rows, col_block, capacity, feature_width)
    at_row = lax.all_to_all(grouped, "dp", split_axis=1, concat_axis=1, tiled=True)
    gathered = at_row[:, None]
    for bit_index in range(SLICES.bit_length() - 1):
        far_rows = swapped(gathered, "dp", bit_index)
        lower_half = slice_here // (1 << bit_index) % 2 == 0
        first_part = jnp.where(lower_half, gathered, far_rows)
        second_part = jnp.where(lower_half, far_rows, gathered)
        gathered = jnp.concatenate([first_part, second_part], axis=1)
    all_rows = gathered.reshape(2, -1, feature_width)
    rows_x = all_rows[0]
    rows_d = all_rows[1]
    gate_and_up = lax.dot_general(
        rows_x, gate_up, contract_last, preferred_element_type=jnp.float32
    )
    gate_pre = gate_and_up[:, :slice_width]
    up_pre = gate_and_up[:, slice_width:]
    activated, slope_of = silu_parts(gate_pre)
    hidden = (activated * up_pre).astype(jnp.bfloat16)
    hidden_grad = lax.dot_general(
        rows_d, down_rows, contract_last, preferred_element_type=jnp.float32
    )
    pre_grads = jnp.concatenate(
        [
            (hidden_grad * up_pre * slope_of).astype(jnp.bfloat16),
            (hidden_grad * activated).astype(jnp.bfloat16),
        ],
        axis=1,
    )
    grad_gu = lax.dot_general(
        pre_grads, rows_x, contract_first, preferred_element_type=jnp.float32
    ).astype(jnp.bfloat16)
    grad_dn = lax.dot_general(
        hidden, rows_d, contract_first, preferred_element_type=jnp.float32
    ).astype(jnp.bfloat16)
    slice_part = jnp.dot(pre_grads, gate_up, preferred_element_type=jnp.float32).astype(
        jnp.bfloat16
    )
    grad_pack = jnp.concatenate([grad_gu, grad_dn], axis=0)
    blocks = slice_part.reshape(2, 2, n_rows, col_block, capacity, feature_width)
    upper_half = slice_here // 2 % 2 == 1
    keep_half = jnp.where(upper_half, blocks[1], blocks[0])
    send_half = jnp.where(upper_half, blocks[0], blocks[1])
    got_half = swapped(send_half, "dp", 1)
    pairsum = keep_half.astype(jnp.float32) + got_half.astype(jnp.float32)
    odd_slice = slice_here % 2 == 1
    keep_last = jnp.where(odd_slice, pairsum[1], pairsum[0])
    send_last = jnp.where(odd_slice, pairsum[0], pairsum[1])
    got_last = swapped(send_last, "dp", 0)
    summed = keep_last + got_last
    back_rows = lax.all_to_all(summed, "dp", split_axis=0, concat_axis=0, tiled=True).reshape(
        slot_count, n_cols, capacity, feature_width
    )
    home_rows = lax.all_to_all(
        back_rows, "expert", split_axis=1, concat_axis=1, tiled=True
    ).reshape(buffer_rows, feature_width)
    hits = (
        target.reshape(tok_dev, top_count)[:, :, None]
        == jnp.arange(buffer_rows, dtype=jnp.int32)[None, None, :]
    )
    gather_mat = jnp.sum(hits.astype(jnp.float32), axis=1)
    grad_tokens = jnp.dot(
        gather_mat, home_rows, precision=lax.Precision.HIGHEST, preferred_element_type=jnp.float32
    ).astype(jnp.bfloat16)
    grad_gate_up = grad_pack[: 2 * slice_width].reshape(w_gate_up.shape)
    grad_down = grad_pack[2 * slice_width :].reshape(w_down.shape)
    return (grad_tokens, grad_gate_up, grad_down)


def solution(mesh):
    return jax.shard_map(
        per_device,
        mesh=mesh,
        in_specs=(
            P(("dp", "expert"), None),
            P(("dp", "expert"), None),
            P(("dp", "expert"), None),
            P(("dp", "expert"), None),
            P(),
            P("expert", "dp", None, None),
            P("expert", "dp", None, None),
        ),
        out_specs=(
            P(("dp", "expert"), None),
            P("expert", "dp", None, None),
            P("expert", "dp", None, None),
        ),
        check_vma=False,
    )
```

profile of v0, /device:TPU:0, one launch (start us, length us, event | category | flops | bytes accessed | tf_op | source)
XLA Modules:
  0.0 155.5 jit_solution(3908190138003010095)
XLA Ops:
  0.6 0.0 copy-start
  0.6 0.8 copy.22
  1.4 0.1 eq.95
  1.5 0.2 convert_reduce_fusion.1
  1.7 0.7 select_reduce_fusion
  2.4 0.8 convert_element_type.69
  3.2 0.8 copy.23
  3.9 0.1 mul.85
  4.1 0.1 fusion.7
  4.2 0.3 convolution_convert_fusion.2
  4.6 21.5 %all_to_all.20 = bf16[2,1,8,16,1024]{4,3,0,1,2:T(8,128)(2,1)S(1)} all-to-all(bf16[2,1,8,16,1024]{4,3,0,1,2:T(8,128)(2,1)S(1)} %copy.24), channel_id=1, replica_groups=mesh['dp'=4,'expert'=8] {'expert'}, dimensions={2} | all-to-all | bytes 1048576 | tf_op jit(solution)/shard_map/all_to_all | solution.py:77
  26.1 0.0 copy-start.2
  26.1 11.8 %all_to_all.21 = bf16[2,4,2,16,1024]{4,3,2,0,1:T(8,128)(2,1)S(1)} all-to-all(bf16[2,4,2,16,1024]{4,3,2,0,1:T(8,128)(2,1)S(1)} %copy.25), channel_id=1, replica_groups=mesh['dp'=4,'expert'=8] {'dp'}, dimensions={1} | all-to-all | bytes 1048576 | tf_op jit(solution)/shard_map/all_to_all | solution.py:85
  37.9 0.9 collective-permute-start
  38.8 0.1 constant_dynamic-update-slice_fusion.1
  38.9 0.1 collective-permute-start.2
  39.0 10.4 %collective-permute-done = bf16[2,1,4,2,16,1024]{5,4,3,0,2,1:T(8,128)(2,1)S(1)} collective-permute-done((bf16[2,1,4,2,16,1024]{5,4,3,0,2,1:T(8,128)(2,1)S(1)}, bf16[2,1,4,2,16,1024]{5,4,3,0,2,1:T(8,128)(2,1)S(1)}, u32[]{:S(2)}, u32[]{:S(2)}) %collective-permute-start) | collective-permute-done | bytes 524320 | tf_op jit(solution)/shard_map/ppermute | solution.py:20
  49.5 0.1 broadcast_select_fusion.4
  49.5 1.1 pad_maximum_fusion.1
  50.6 1.5 collective-permute-start.1
  52.1 0.6 fusion.21
  53.4 37.3 %collective-permute-done.2 = bf16[1,1,576,1024]{3,2,1,0:T(8,128)(2,1)} collective-permute-done((bf16[1,1,576,1024]{3,2,1,0:T(8,128)(2,1)S(1)}, bf16[1,1,576,1024]{3,2,1,0:T(8,128)(2,1)}, u32[]{:S(2)}, u32[]{:S(2)}) %collective-permute-start.2) | collective-permute-done | bytes 1179680 | tf_op jit(solution)/shard_map/ppermute | solution.py:20
  90.7 0.1 broadcast_select_fusion
  90.8 0.1 broadcast_select_fusion.1
  91.0 0.2 pad_maximum_fusion
  91.2 0.6 fusion.3
  91.8 0.6 multiply_convert_fusion.2
  92.4 0.3 copy-done.6
  92.7 0.7 copy-done.4
  93.4 0.7 convolution_convert_fusion
  94.1 0.1 broadcast_select_fusion.5
  94.2 1.0 collective-permute-start.3
  95.1 13.7 %collective-permute-done.3 = bf16[2,4,2,16,1024]{4,3,2,1,0:T(8,128)(2,1)} collective-permute-done((bf16[2,4,2,16,1024]{4,3,2,1,0:T(8,128)(2,1)S(1)}, bf16[2,4,2,16,1024]{4,3,2,1,0:T(8,128)(2,1)}, u32[]{:S(2)}, u32[]{:S(2)}) %collective-permute-start.3) | collective-permute-done | bytes 524320 | tf_op jit(solution)/shard_map/ppermute | solution.py:20
  108.8 1.2 convert_add_fusion
  110.0 0.1 select_bitcast_fusion
  110.1 0.9 collective-permute-start.4
  111.0 13.1 %collective-permute-done.4 = f32[4,2,16,1024]{3,2,1,0:T(8,128)S(1)} collective-permute-done((f32[4,2,16,1024]{3,2,1,0:T(8,128)S(1)}, f32[4,2,16,1024]{3,2,1,0:T(8,128)S(1)}, u32[]{:S(2)}, u32[]{:S(2)}) %collective-permute-start.4) | collective-permute-done | bytes 524320 | tf_op jit(solution)/shard_map/ppermute | solution.py:20
  124.1 0.1 bitcast_add_fusion
  124.3 11.5 %all_to_all.22 = f32[4,2,16,1024]{3,2,1,0:T(8,128)} all-to-all(f32[4,2,16,1024]{3,2,1,0:T(8,128)S(1)} %bitcast_add_fusion), channel_id=1, replica_groups=mesh['dp'=4,'expert'=8] {'dp'}, dimensions={0} | all-to-all | bytes 1048576 | tf_op jit(solution)/shard_map/all_to_all | solution.py:134
  135.8 3.5 %all-to-all-start.3 = ((f32[1,8,16,1024]{3,2,0,1:T(8,128)}), f32[1,8,16,1024]{3,2,0,1:T(8,128)S(1)}, u32[]{:S(2)}, u32[]{:S(2)}) async-start(f32[1,8,16,1024]{3,2,0,1:T(8,128)} %bitcast.16), calls=%async_computation.3 | async-start | bytes 1048576 | tf_op jit(solution)/shard_map/all_to_all | solution.py:137
  139.3 0.1 reduce_sum.40
  139.3 0.1 mul.81
  139.4 0.0 copy-start.7
  139.4 0.1 convert_reduce_fusion
  139.6 1.5 fusion
  141.0 1.2 fusion.1
  142.2 12.4 %all-to-all-done.3 = f32[1,8,16,1024]{3,2,0,1:T(8,128)S(1)} async-done(((f32[1,8,16,1024]{3,2,0,1:T(8,128)}), f32[1,8,16,1024]{3,2,0,1:T(8,128)S(1)}, u32[]{:S(2)}, u32[]{:S(2)}) %all-to-all-start.3) | async-done | bytes 524320 | tf_op jit(solution)/shard_map/all_to_all | solution.py:137
  154.5 1.0 convolution_convert_fusion.4
  (18 shorter events, 0.2 us)
Async XLA Ops:
  0.6 3.4 %copy-start = (bf16[16,1024]{1,0:T(8,128)(2,1)S(1)}, bf16[16,1024]{1,0:T(8,128)(2,1)}, u32[]{:S(2)}) copy-start(bf16[16,1024]{1,0:T(8,128)(2,1)} %param.7) | copy-start | bytes 98308
  26.0 12.8 %copy-start.1 = (bf16[1,1,384,1024]{3,2,1,0:T(8,128)(2,1)S(1)}, bf16[1,1,384,1024]{3,2,1,0:T(8,128)(2,1)}, u32[]{:S(2)}) copy-start(bf16[1,1,384,1024]{3,2,1,0:T(8,128)(2,1)} %param.12) | copy-start | bytes 2359300
  26.1 12.8 %copy-start.2 = (bf16[1,1,192,1024]{3,2,1,0:T(8,128)(2,1)S(1)}, bf16[1,1,192,1024]{3,2,1,0:T(8,128)(2,1)}, u32[]{:S(2)}) copy-start(bf16[1,1,192,1024]{3,2,1,0:T(8,128)(2,1)} %param.13) | copy-start | bytes 1179652
  37.9 11.5 %collective-permute-start = (bf16[2,1,4,2,16,1024]{5,4,3,0,2,1:T(8,128)(2,1)S(1)}, bf16[2,1,4,2,16,1024]{5,4,3,0,2,1:T(8,128)(2,1)S(1)}, u32[]{:S(2)}, u32[]{:S(2)}) collective-permute-start(bf16[2,1,4,2,16,1024]{5,4,3,0,2,1:T(8,128)(2,1)S(1)} %bitcast.47), channel_id=1, source_target_pairs={{0,8},{8,0},{16,24},{24,16},{1,9},{9,1},{17,25},{25,17},{2,10},{10... | collective-permute-start | bytes 1572872 | tf_op jit(solution)/shard_map/ppermute | solution.py:20
  38.9 51.8 %collective-permute-start.2 = (bf16[1,1,576,1024]{3,2,1,0:T(8,128)(2,1)S(1)}, bf16[1,1,576,1024]{3,2,1,0:T(8,128)(2,1)}, u32[]{:S(2)}, u32[]{:S(2)}) collective-permute-start(bf16[1,1,576,1024]{3,2,1,0:T(8,128)(2,1)S(1)} %constant_dynamic-update-slice_fusion), channel_id=1, source_target_pairs={{0,4},{4,0},{1,5},{5,1},{2,6},{6,2},{3,7},{7,3},{8,12},{12,8},{9,1... | collective-permute-start | bytes 3538952 | tf_op jit(solution)/shard_map/ppermute | solution.py:20
  49.5 2.6 %copy-start.3 = (s32[8,1]{0,1:T(1,128)S(1)}, s32[8,1]{0,1:T(1,128)}, u32[]{:S(2)}) copy-start(s32[8,1]{0,1:T(1,128)} %param.11) | copy-start | bytes 100
  50.6 40.2 %collective-permute-start.1 = (bf16[2,2,4,2,16,1024]{5,4,3,0,2,1:T(8,128)(2,1)}, bf16[2,2,4,2,16,1024]{5,4,3,0,2,1:T(8,128)(2,1)S(1)}, u32[]{:S(2)}, u32[]{:S(2)}) collective-permute-start(bf16[2,2,4,2,16,1024]{5,4,3,0,2,1:T(8,128)(2,1)} %pad_maximum_fusion.1), channel_id=1, source_target_pairs={{0,16},{16,0},{8,24},{24,8},{1,17},{17,1},{9,25},{25,9},{2,18},{18... | collective-permute-start | bytes 3145736 | tf_op jit(solution)/shard_map/ppermute | solution.py:20
  91.8 0.9 copy-start.6
  92.7 0.7 copy-start.4
  94.2 14.7 %collective-permute-start.3 = (bf16[2,4,2,16,1024]{4,3,2,1,0:T(8,128)(2,1)S(1)}, bf16[2,4,2,16,1024]{4,3,2,1,0:T(8,128)(2,1)}, u32[]{:S(2)}, u32[]{:S(2)}) collective-permute-start(bf16[2,4,2,16,1024]{4,3,2,1,0:T(8,128)(2,1)S(1)} %bitcast.56), channel_id=1, source_target_pairs={{0,16},{16,0},{8,24},{24,8},{1,17},{17,1},{9,25},{25,9},{2,18},{18... | collective-permute-start | bytes 1572872 | tf_op jit(solution)/shard_map/ppermute | solution.py:20
  110.1 14.0 %collective-permute-start.4 = (f32[4,2,16,1024]{3,2,1,0:T(8,128)S(1)}, f32[4,2,16,1024]{3,2,1,0:T(8,128)S(1)}, u32[]{:S(2)}, u32[]{:S(2)}) collective-permute-start(f32[4,2,16,1024]{3,2,1,0:T(8,128)S(1)} %select_bitcast_fusion), channel_id=1, source_target_pairs={{0,8},{8,0},{16,24},{24,16},{1,9},{9,1},{17,25},{25,17},{2,10},{10... | collective-permute-start | bytes 1572872 | tf_op jit(solution)/shard_map/ppermute | solution.py:20
  124.2 15.3 %copy-start.5 = (bf16[512,192]{0,1:T(8,128)(2,1)S(1)}, bf16[512,192]{0,1:T(8,128)(2,1)}, u32[]{:S(2)}) copy-start(bf16[512,192]{0,1:T(8,128)(2,1)} %copy-done.4) | copy-start | bytes 589828
  135.8 18.8 %all-to-all-start.3 = ((f32[1,8,16,1024]{3,2,0,1:T(8,128)}), f32[1,8,16,1024]{3,2,0,1:T(8,128)S(1)}, u32[]{:S(2)}, u32[]{:S(2)}) async-start(f32[1,8,16,1024]{3,2,0,1:T(8,128)} %bitcast.16), calls=%async_computation.3 | async-start | bytes 1048576 | tf_op jit(solution)/shard_map/all_to_all | solution.py:137
  139.4 1.6 %copy-start.7 = (f32[512,384]{0,1:T(8,128)S(1)}, f32[512,384]{0,1:T(8,128)}, u32[]{:S(2)}) copy-start(f32[512,384]{0,1:T(8,128)} %copy-done.6) | copy-start | bytes 2359300
where the time goes:
time: 155 us; the launch traced here: 156 us
  waiting for transfers between devices  86.9 us (56%)
  blocking collectives  44.8 us (29%)
  starting transfers between devices  7.83 us (5%)
  matrix products  5.81 us (4%)
  other arithmetic  5.59 us (4%)
  local copies, waits for them, and re-layouts  3.06 us (2%)
  between operations  1.58 us (1%)
    ppermute x5, waiting for transfers between devices, swapped(): return lax.ppermute(block, axis, route)  74.5 us
    all_to_all x1, blocking collectives, per_device(): lax.all_to_all(sent, 'expert', split_axis=2, concat_axis=2, tiled=True)  21.5 us
    all_to_all x1, waiting for transfers between devices, per_device(): lax.all_to_all(back_rows, 'expert', split_axis=1, concat_axis=1, tiled=True)  12.4 us
    all_to_all x1, blocking collectives, per_device(): lax.all_to_all(grouped, 'dp', split_axis=1, concat_axis=1, tiled=True)  11.8 us
    all_to_all x1, blocking collectives, per_device(): lax.all_to_all(summed, 'dp', split_axis=0, concat_axis=0, tiled=True)  11.5 us
    ppermute x5, starting transfers between devices, swapped(): return lax.ppermute(block, axis, route)  4.33 us
    all_to_all x1, starting transfers between devices, per_device(): lax.all_to_all(back_rows, 'expert', split_axis=1, concat_axis=1, tiled=True)  3.49 us
  transfers between devices with their start and end apart: 6, of which 5 were waited for; matrix products, arithmetic and copies ran while one was open for 3% of the time, Pallas kernels for 0%

commit v1 on v0

--- a/solution.py
+++ b/solution.py
@@ -1,6 +1,10 @@
+import functools
+
 import jax
 import jax.numpy as jnp
 from jax import lax
+from jax.experimental import pallas as pl
+from jax.experimental.pallas import tpu as pltpu
 from jax.sharding import PartitionSpec as P
 
 SLICES = 4
@@ -31,7 +35,7 @@
     return jnp.sum(jnp.where(rows_hit & cols_hit, lookup_table, 0))
 
 
-def per_device(tokens, upstream, expert_ids, gates, relocate, w_gate_up, w_down):
+def routed_device(tokens, upstream, expert_ids, gates, relocate, w_gate_up, w_down):
     n_rows = lax.axis_size("dp")
     n_cols = lax.axis_size("expert")
     slot_count = n_rows // SLICES
@@ -150,7 +154,170 @@
     return (grad_tokens, grad_gate_up, grad_down)
 
 
+def crossed(block, axis, apart):
+    return lax.ppermute(block, axis, [(i, i ^ apart) for i in range(lax.axis_size(axis))])
+
+
+def whole(count):
+    return [pl.BlockSpec(memory_space=pltpu.VMEM)] * count
+
+
+def pack_kernel(n_cols, ids_ref, gates_ref, tokens_ref, upstream_ref, packed_ref):
+    width = tokens_ref.shape[1]
+    lane = lax.broadcasted_iota(jnp.int32, (tokens_ref.shape[0], 128), 1)
+    table = jnp.zeros(lane.shape, jnp.float32)
+    for k in range(ids_ref.shape[1]):
+        table += jnp.where(ids_ref[:, k : k + 1] == lane % n_cols, gates_ref[:, k : k + 1], 0.0)
+    high = table.astype(jnp.bfloat16)
+    rest = table - high.astype(jnp.float32)
+    middle = rest.astype(jnp.bfloat16)
+    low = (rest - middle.astype(jnp.float32)).astype(jnp.bfloat16)
+    zero = jnp.zeros_like(high)
+    part = lane // n_cols
+    packed_ref[:, :width] = tokens_ref[...]
+    packed_ref[:, width : 2 * width] = upstream_ref[...]
+    packed_ref[:, 2 * width :] = jnp.where(
+        part == 0, high, jnp.where(part == 1, middle, jnp.where(part == 2, low, zero))
+    )
+
+
+def forward_kernel(n_cols, n_rows, tok_dev, plane_ref, wgu_own, wdn_own, wgu_sib, wdn_sib, own_ref, sib_ref, kept_ref, *sent_refs):
+    units, width = wdn_own.shape
+    col_here = lax.axis_index("expert")
+    lane = lax.broadcasted_iota(jnp.int32, (8, 128), 1)
+    row = lax.broadcasted_iota(jnp.int32, (8, 128), 0)
+    wanted = jnp.where(row == 0, col_here, col_here ^ 1)
+    chosen = (row < 2) & (lane % n_cols == wanted) & (lane < 3 * n_cols)
+    gate_rows = lax.dot_general(
+        jnp.where(chosen, 1.0, 0.0).astype(jnp.bfloat16), plane_ref[:, 2 * width :], contract_last, preferred_element_type=jnp.float32
+    )
+    total = None
+    for index, (wgu, wdn, acts_ref) in enumerate(((wgu_own, wdn_own, own_ref), (wgu_sib, wdn_sib, sib_ref))):
+        gate = gate_rows[index : index + 1, :]
+        pre = lax.dot_general(wgu[...], plane_ref[:, :width], contract_last, preferred_element_type=jnp.float32)
+        hidden_grad = gate * lax.dot_general(
+            wdn[...], plane_ref[:, width : 2 * width], contract_last, preferred_element_type=jnp.float32
+        )
+        activated, slope_of = silu_parts(pre[:units])
+        up_pre = pre[units:]
+        acts_ref[:units] = (hidden_grad * up_pre * slope_of).astype(jnp.bfloat16)
+        acts_ref[units : 2 * units] = (hidden_grad * activated).astype(jnp.bfloat16)
+        acts_ref[2 * units :] = (activated * up_pre * gate).astype(jnp.bfloat16)
+        part = lax.dot_general(acts_ref[: 2 * units], wgu[...], contract_first, preferred_element_type=jnp.float32)
+        total = part if total is None else total + part
+    for z in range(plane_ref.shape[0] // (n_rows * tok_dev)):
+        for d in range(n_rows):
+            start = (z * n_rows + d) * tok_dev
+            block = total[start : start + tok_dev]
+            if d == 0:
+                kept_ref[z] = block
+            else:
+                sent_refs[d - 1][z] = block.astype(jnp.bfloat16)
+
+
+def weight_grad_kernel(relocate_ref, same_ref, cross_ref, plane_ref, other_ref, gu_ref, dn_ref):
+    units, width = dn_ref.shape
+    half = plane_ref.shape[0] // 2
+    first = pl.multiple_of(relocate_ref[lax.axis_index("expert"), 0] * half, half)
+    for acts, rows_ref, start in ((same_ref, plane_ref, True), (cross_ref, other_ref, False)):
+        for side in range(2):
+            rows = pl.ds(first if side == 0 else half - first, half)
+            lanes = slice(side * half, (side + 1) * half)
+            gu = jnp.dot(acts[: 2 * units, lanes], rows_ref[rows, :width], preferred_element_type=jnp.float32)
+            dn = jnp.dot(acts[2 * units :, lanes], rows_ref[rows, width : 2 * width], preferred_element_type=jnp.float32)
+            if start and side == 0:
+                gu_sum, dn_sum = gu, dn
+            else:
+                gu_sum, dn_sum = gu_sum + gu, dn_sum + dn
+    gu_ref[...] = gu_sum.astype(jnp.bfloat16)
+    dn_ref[...] = dn_sum.astype(jnp.bfloat16)
+
+
+def exchanges(pattern, acts_own, acts_sib, plane, sent_rows):
+    n_cols = lax.axis_size("expert")
+    half = n_cols // 2
+
+    def place(col):
+        return col ^ half if pattern >> (col % half) & 1 else col
+
+    got_same = lax.ppermute(acts_own, "expert", [(col, place(col)) for col in range(n_cols)])
+    got = [crossed(block, "dp", d + 1) for d, block in enumerate(sent_rows)]
+    plane_sib = crossed(plane, "expert", 1)
+    got_cross = lax.ppermute(acts_sib, "expert", [(col, place(col ^ 1)) for col in range(n_cols)])
+    return got_same, got_cross, plane_sib, got
+
+
+def dense_device(tokens, upstream, expert_ids, gates, relocate, w_gate_up, w_down):
+    n_rows = lax.axis_size("dp")
+    n_cols = lax.axis_size("expert")
+    n_z = n_cols // 2
+    tok_dev = tokens.shape[0]
+    half = n_cols // 2
+    units, width = w_down.shape[2:]
+    plane_rows = n_rows * n_z * tok_dev
+    limit = pltpu.CompilerParams(vmem_limit_bytes=48 * 2**20)
+    bf16 = jnp.bfloat16
+
+    own = pl.pallas_call(
+        functools.partial(pack_kernel, n_cols),
+        out_shape=jax.ShapeDtypeStruct((tok_dev, 2 * width + 128), bf16),
+        in_specs=whole(4),
+        out_specs=whole(1)[0],
+        compiler_params=limit,
+        name="pack",
+    )(expert_ids, gates, tokens, upstream)
+
+    along_dp = [crossed(own, "dp", d) for d in range(1, n_rows)]
+    along_z = [crossed(own, "expert", 2 * dz) for dz in range(1, n_z)]
+    bits = jnp.sum(relocate[:half, 0] << jnp.arange(half, dtype=jnp.int32))
+    along_z, along_dp, w_gate_up, w_down, bits = lax.optimization_barrier((along_z, along_dp, w_gate_up, w_down, bits))
+    far = jnp.concatenate(along_z, axis=0)
+    far_dp = [crossed(far, "dp", d) for d in range(1, n_rows)]
+    wgu_own, wdn_own = w_gate_up[0, 0], w_down[0, 0]
+    wgu_sib = crossed(wgu_own, "expert", 1)
+    wdn_sib = crossed(wdn_own, "expert", 1)
+    plane = [own] + along_dp
+    for dz in range(n_z - 1):
+        plane += [along_z[dz]] + [block[dz * tok_dev : (dz + 1) * tok_dev] for block in far_dp]
+    plane = jnp.concatenate(plane, axis=0)
+
+    acts = jax.ShapeDtypeStruct((3 * units, plane_rows), bf16)
+    acts_own, acts_sib, kept, *sent = pl.pallas_call(
+        functools.partial(forward_kernel, n_cols, n_rows, tok_dev),
+        out_shape=[acts, acts, jax.ShapeDtypeStruct((n_z, tok_dev, width), jnp.float32)]
+        + [jax.ShapeDtypeStruct((n_z, tok_dev, width), bf16)] * (n_rows - 1),
+        in_specs=whole(5),
+        out_specs=whole(2 + n_rows),
+        compiler_params=limit,
+        name="forward",
+    )(plane, wgu_own, wdn_own, wgu_sib, wdn_sib)
+
+    branches = [functools.partial(exchanges, pattern) for pattern in range(1, (1 << half) - 1)]
+    got_same, got_cross, plane_sib, got = lax.switch(bits - 1, branches, acts_own, acts_sib, plane, sent)
+    total = kept
+    for block in got:
+        total = total + block.astype(jnp.float32)
+    sent_total = total.astype(bf16)
+    grad_tokens = total[0]
+    for dz in range(1, n_z):
+        grad_tokens = grad_tokens + crossed(sent_total[dz], "expert", 2 * dz).astype(jnp.float32)
+    grad_gu, grad_dn = pl.pallas_call(
+        weight_grad_kernel,
+        out_shape=[jax.ShapeDtypeStruct((2 * units, width), bf16), jax.ShapeDtypeStruct((units, width), bf16)],
+        in_specs=[pl.BlockSpec(memory_space=pltpu.SMEM)] + whole(4),
+        out_specs=whole(2),
+        compiler_params=limit,
+        name="weight_grads",
+    )(relocate, got_same, got_cross, plane, plane_sib)
+    return grad_tokens.astype(bf16), grad_gu.reshape(w_gate_up.shape), grad_dn.reshape(w_down.shape)
+
+
 def solution(mesh):
+    def per_device(*arrays):
+        n_rows, n_cols = mesh.shape["dp"], mesh.shape["expert"]
+        dense = n_rows == SLICES and arrays[2].shape[1] == n_cols and 4 <= n_cols <= 8
+        return (dense_device if dense else routed_device)(*arrays)
+
     return jax.shard_map(
         per_device,
         mesh=mesh,

time: 155 us -> 68.5 us (0.44)
  waiting for transfers between devices: 86.9 us -> 18.2 us
  blocking collectives: 44.8 us -> 0 us
  starting transfers between devices: 7.83 us -> 25.9 us
  local copies, waits for them, and re-layouts: 3.06 us -> 13.3 us
  Pallas kernels: 0 us -> 6.87 us
  matrix products: 5.81 us -> 0 us
  other arithmetic: 5.59 us -> 3.02 us
    ppermute x5 -> x20, waiting for transfers between devices: 74.5 us -> 18.2 us  [the longest x18 16.9 us: crossed(): lax.ppermute(block, axis, [(i, i ^ apart) for i in range(lax.axis_size(ax...]
    all_to_all x3 -> x0, blocking collectives: 44.8 us -> none  [the longest x1 21.5 us: per_device(): lax.all_to_all(sent, 'expert', split_axis=2, concat_axis=2, tiled=True)]
    ppermute x5 -> x20, starting transfers between devices: 4.33 us -> 25.9 us  [the longest x18 21.2 us: crossed(): lax.ppermute(block, axis, [(i, i ^ apart) for i in range(lax.axis_size(ax...]
    all_to_all x1 -> x0, waiting for transfers between devices: 12.4 us -> none  [per_device(): lax.all_to_all(back_rows, 'expert', split_axis=1, concat_axis=1, tiled=True)]
    unnamed x19 -> x33, local copies, waits for them, and re-layouts: 2.59 us -> 12.7 us
    pallas_call x0 -> x3, Pallas kernels: none -> 6.87 us  [the longest x1 3.73 us: dense_device(): pl.pallas_call(weight_grad_kernel, out_shape=[jax.ShapeDtypeStruct((2 * u...]
    dot_general x7 -> x0, matrix products: 5.81 us -> none  [the longest x1 1.46 us: per_device(): lax.dot_general(pre_grads, rows_x, contract_first, preferred_element_type...]
    all_to_all x1 -> x0, starting transfers between devices: 3.49 us -> none  [per_device(): lax.all_to_all(back_rows, 'expert', split_axis=1, concat_axis=1, tiled=True)]
  transfers between devices with their start and end apart: 6 -> 20, of which waited for: 5 -> 8; matrix products, arithmetic and copies ran while one was open for 3% -> 13% of each run, Pallas kernels for 0% -> 5%
where the time goes in v1:
time: 68.5 us; the launch traced here: 68.8 us
  starting transfers between devices  25.9 us (38%)
  waiting for transfers between devices  18.2 us (27%)
  local copies, waits for them, and re-layouts  13.3 us (19%)
  Pallas kernels  6.87 us (10%)
  other arithmetic  3.02 us (4%)
  between operations  1.4 us (2%)
    ppermute x18, starting transfers between devices, crossed(): lax.ppermute(block, axis, [(i, i ^ apart) for i in range(lax.axis_size(ax...  21.2 us
    ppermute x18, waiting for transfers between devices, crossed(): lax.ppermute(block, axis, [(i, i ^ apart) for i in range(lax.axis_size(ax...  16.9 us
    unnamed x33, local copies, waits for them, and re-layouts  12.7 us
    pallas_call x1, Pallas kernels, dense_device(): pl.pallas_call(weight_grad_kernel, out_shape=[jax.ShapeDtypeStruct((2 * u...  3.73 us
    ppermute x1, starting transfers between devices, exchanges(): lax.ppermute(acts_own, 'expert', [(col, place(col)) for col in range(n_co...  3.56 us
    pallas_call x1, Pallas kernels, dense_device(): pl.pallas_call(functools.partial(forward_kernel, n_cols, n_rows, tok_dev)...  3.02 us
  transfers between devices with their start and end apart: 20, of which 8 were waited for; matrix products, arithmetic and copies ran while one was open for 13% of the time, Pallas kernels for 5%

profile of v1, /device:TPU:0, one launch (start us, length us, event | category | flops | bytes accessed | tf_op | source)
XLA Modules:
  0.0 68.8 jit_solution(14745939524809766606)
XLA Ops:
  0.7 0.9 %copy.10.ids_ref = s32[16,8]{1,0:T(8,128)S(1)} copy(s32[16,8]{0,1:T(8,128)} %param.23) | data formatting | bytes 1024 | tf_op args[2]
  1.5 0.8 %copy.11.gates_ref = f32[16,8]{1,0:T(8,128)S(1)} copy(f32[16,8]{0,1:T(8,128)} %param.24) | data formatting | bytes 1024 | tf_op args[3]
  2.3 0.8 %copy-done.2 = bf16[16,1024]{1,0:T(8,128)(2,1)S(1)} copy-done((bf16[16,1024]{1,0:T(8,128)(2,1)S(1)}, bf16[16,1024]{1,0:T(8,128)(2,1)}, u32[]{:S(2)}) %copy-start.2) | copy-done | bytes 32792
  3.0 0.8 %copy-done.3 = bf16[16,1024]{1,0:T(8,128)(2,1)S(1)} copy-done((bf16[16,1024]{1,0:T(8,128)(2,1)S(1)}, bf16[16,1024]{1,0:T(8,128)(2,1)}, u32[]{:S(2)}) %copy-start.3) | copy-done | bytes 32792
  3.9 3.1 %collective-permute-start.84 = (bf16[16,2176]{1,0:T(8,128)(2,1)S(1)}, bf16[16,2176]{1,0:T(8,128)(2,1)S(1)}, u32[]{:S(2)}, u32[]{:S(2)}) collective-permute-start(bf16[16,2176]{1,0:T(8,128)(2,1)S(1)} %pack.1), channel_id=1, source_target_pairs={{0,2},{1,3},{2,0},{3,1},{4,6},{5,7},{6,4},{7,5},{8,10},{9,11},{10,... | collective-permute-start | bytes 208904 | tf_op jit(solution)/shard_map/ppermute | solution.py:158
  7.0 2.6 %collective-permute-start.85 = (bf16[16,2176]{1,0:T(8,128)(2,1)S(1)}, bf16[16,2176]{1,0:T(8,128)(2,1)S(1)}, u32[]{:S(2)}, u32[]{:S(2)}) collective-permute-start(bf16[16,2176]{1,0:T(8,128)(2,1)S(1)} %pack.1), channel_id=1, source_target_pairs={{0,4},{1,5},{2,6},{3,7},{4,0},{5,1},{6,2},{7,3},{8,12},{9,13},{10,... | collective-permute-start | bytes 208904 | tf_op jit(solution)/shard_map/ppermute | solution.py:158
  9.6 1.7 %collective-permute-start.87 = (bf16[16,2176]{1,0:T(8,128)(2,1)S(1)}, bf16[16,2176]{1,0:T(8,128)(2,1)S(1)}, u32[]{:S(2)}, u32[]{:S(2)}) collective-permute-start(bf16[16,2176]{1,0:T(8,128)(2,1)S(1)} %pack.1), channel_id=1, source_target_pairs={{0,8},{8,0},{16,24},{24,16},{1,9},{9,1},{17,25},{25,17},{2,10},{10... | collective-permute-start | bytes 208904 | tf_op jit(solution)/shard_map/ppermute | solution.py:158
  11.3 1.5 %collective-permute-start.88 = (bf16[16,2176]{1,0:T(8,128)(2,1)S(1)}, bf16[16,2176]{1,0:T(8,128)(2,1)S(1)}, u32[]{:S(2)}, u32[]{:S(2)}) collective-permute-start(bf16[16,2176]{1,0:T(8,128)(2,1)S(1)} %pack.1), channel_id=1, source_target_pairs={{0,16},{8,24},{16,0},{24,8},{1,17},{9,25},{17,1},{25,9},{2,18},{10... | collective-permute-start | bytes 208904 | tf_op jit(solution)/shard_map/ppermute | solution.py:158
  12.8 0.6 constant_dynamic-update-slice_fusion.9
  13.7 1.3 %fusion.4 = s32[]{:T(128)} fusion(s32[8,1]{0,1:T(1,128)} %param.25), kind=kLoop, calls=%fused_computation.31 | loop fusion | flops 7 | bytes 20 | tf_op jit(solution)/shard_map/reduce_sum | solution.py:272
  15.0 0.8 %collective-permute-done.86 = bf16[16,2176]{1,0:T(8,128)(2,1)S(1)} collective-permute-done((bf16[16,2176]{1,0:T(8,128)(2,1)S(1)}, bf16[16,2176]{1,0:T(8,128)(2,1)S(1)}, u32[]{:S(2)}, u32[]{:S(2)}) %collective-permute-start.86) | collective-permute-done | bytes 69664 | tf_op jit(solution)/shard_map/ppermute | solution.py:158
  15.8 0.6 collective-permute-done.88
  16.3 2.3 %collective-permute-done.89 = bf16[16,2176]{1,0:T(8,128)(2,1)S(1)} collective-permute-done((bf16[16,2176]{1,0:T(8,128)(2,1)S(1)}, bf16[16,2176]{1,0:T(8,128)(2,1)S(1)}, u32[]{:S(2)}, u32[]{:S(2)}) %collective-permute-start.89) | collective-permute-done | bytes 69664 | tf_op jit(solution)/shard_map/ppermute | solution.py:158
  18.7 0.6 constant_dynamic-update-slice_fusion.8
  19.3 0.6 constant_dynamic-update-slice_fusion.7
  19.9 0.6 constant_dynamic-update-slice_fusion.6
  20.5 0.6 constant_dynamic-update-slice_fusion.2
  21.2 0.6 collective-permute-start.90
  22.1 2.7 %collective-permute-start.92 = (bf16[48,2176]{1,0:T(8,128)(2,1)S(1)}, bf16[48,2176]{1,0:T(8,128)(2,1)S(1)}, u32[]{:S(2)}, u32[]{:S(2)}) collective-permute-start(bf16[48,2176]{1,0:T(8,128)(2,1)S(1)} %constant_dynamic-update-slice_fusion), channel_id=1, source_target_pairs={{0,24},{8,16},{16,8},{24,0},{1,25},{9,17},{17,9},{25,1},{2,26},{10... | collective-permute-start | bytes 626696 | tf_op jit(solution)/shard_map/ppermute | solution.py:158
  24.7 0.5 collective-permute-start.94
  25.9 2.1 %collective-permute-done.90 = bf16[48,2176]{1,0:T(8,128)(2,1)S(1)} collective-permute-done((bf16[48,2176]{1,0:T(8,128)(2,1)S(1)}, bf16[48,2176]{1,0:T(8,128)(2,1)S(1)}, u32[]{:S(2)}, u32[]{:S(2)}) %collective-permute-start.90) | collective-permute-done | bytes 208928 | tf_op jit(solution)/shard_map/ppermute | solution.py:158
  28.0 0.6 slice_dynamic-update-slice_fusion.8
  28.7 2.5 %collective-permute-done.91 = bf16[48,2176]{1,0:T(8,128)(2,1)S(1)} collective-permute-done((bf16[48,2176]{1,0:T(8,128)(2,1)S(1)}, bf16[48,2176]{1,0:T(8,128)(2,1)S(1)}, u32[]{:S(2)}, u32[]{:S(2)}) %collective-permute-start.91) | collective-permute-done | bytes 208928 | tf_op jit(solution)/shard_map/ppermute | solution.py:158
  31.2 0.6 slice_dynamic-update-slice_fusion.7
  31.8 0.6 slice_dynamic-update-slice_fusion.6
  32.4 0.6 constant_dynamic-update-slice_fusion.4
  33.0 0.6 slice_dynamic-update-slice_fusion.5
  33.7 0.6 slice_dynamic-update-slice_fusion.4
  34.3 0.6 slice_dynamic-update-slice_fusion.3
  34.9 0.6 constant_dynamic-update-slice_fusion.3
  35.5 0.6 slice_dynamic-update-slice_fusion.2
  36.2 0.6 slice_dynamic-update-slice_fusion.1
  36.8 0.6 slice_dynamic-update-slice_fusion.plane_ref
  37.5 3.0 %forward.1 = (bf16[576,256]{1,0:T(8,128)(2,1)S(1)}, bf16[576,256]{1,0:T(8,128)(2,1)S(1)}, f32[4,16,1024]{2,1,0:T(8,128)S(1)}, bf16[4,16,1024]{2,1,0:T(8,128)(2,1...) custom-call(bf16[256,2176]{1,0:T(8,128)(2,1)} %slice_dynamic-update-slice_fusion.plane_ref, ...), custom_call_target="tpu_custom_call" | custom-call | tf_op jit(solution)/shard_map/forward/pallas_call | solution.py:285
  40.5 18.2 %conditional.4 = (bf16[576,256]{1,0:T(8,128)(2,1)}, bf16[576,256]{1,0:T(8,128)(2,1)}, bf16[256,2176]{1,0:T(8,128)(2,1)}, bf16[4,16,1024]{2,1,0:T(8,128)(2,1)}, b...) conditional(s32[]{:T(128)} %clamp.3, (bf16[576,256]{1,0:T(8,128)(2,1)S(1)}, ...), branch_computations={%region_1.0_spmd, %region_2.0_spmd, %region_3.0_spmd, %region_4.0_... | conditional | bytes 8388896
  40.6 3.6 %collective-permute-start.12 = (bf16[576,256]{1,0:T(8,128)(2,1)S(1)}, bf16[576,256]{1,0:T(8,128)(2,1)}, u32[]{:S(2)}, u32[]{:S(2)}) collective-permute-start(bf16[576,256]{1,0:T(8,128)(2,1)S(1)} %get-tuple-element.204), channel_id=1, source_target_pairs={{0,4},{1,5},{2,2},{3,3},{4,0},{5,1},{6,6},{7,7},{8,12},{9,13},{10,... | collective-permute-start | bytes 884744 | tf_op jit(solution)/shard_map/cond/branch_2_fun/ppermute | solution.py:243
  44.2 1.1 %collective-permute-start.13 = (bf16[576,256]{1,0:T(8,128)(2,1)S(1)}, bf16[576,256]{1,0:T(8,128)(2,1)}, u32[]{:S(2)}, u32[]{:S(2)}) collective-permute-start(bf16[576,256]{1,0:T(8,128)(2,1)S(1)} %get-tuple-element.205), channel_id=1, source_target_pairs={{0,5},{1,4},{2,3},{3,2},{4,1},{5,0},{6,7},{7,6},{8,13},{9,12},{10,... | collective-permute-start | bytes 884744 | tf_op jit(solution)/shard_map/cond/branch_2_fun/ppermute | solution.py:246
  45.4 1.0 %collective-permute-start.15 = (bf16[4,16,1024]{2,1,0:T(8,128)(2,1)S(1)}, bf16[4,16,1024]{2,1,0:T(8,128)(2,1)}, u32[]{:S(2)}, u32[]{:S(2)}) collective-permute-start(bf16[4,16,1024]{2,1,0:T(8,128)(2,1)S(1)} %get-tuple-element.207), channel_id=1, source_target_pairs={{0,8},{8,0},{16,24},{24,16},{1,9},{9,1},{17,25},{25,17},{2,10},{10... | collective-permute-start | bytes 393224 | tf_op jit(solution)/shard_map/cond/branch_2_fun/ppermute | solution.py:158
  46.4 1.0 %collective-permute-start.16 = (bf16[4,16,1024]{2,1,0:T(8,128)(2,1)S(1)}, bf16[4,16,1024]{2,1,0:T(8,128)(2,1)}, u32[]{:S(2)}, u32[]{:S(2)}) collective-permute-start(bf16[4,16,1024]{2,1,0:T(8,128)(2,1)S(1)} %get-tuple-element.208), channel_id=1, source_target_pairs={{0,16},{8,24},{16,0},{24,8},{1,17},{9,25},{17,1},{25,9},{2,18},{10... | collective-permute-start | bytes 393224 | tf_op jit(solution)/shard_map/cond/branch_2_fun/ppermute | solution.py:158
  47.3 4.0 %collective-permute-done.15 = bf16[4,16,1024]{2,1,0:T(8,128)(2,1)} collective-permute-done((bf16[4,16,1024]{2,1,0:T(8,128)(2,1)S(1)}, bf16[4,16,1024]{2,1,0:T(8,128)(2,1)}, u32[]{:S(2)}, u32[]{:S(2)}) %collective-permute-start.15) | collective-permute-done | bytes 131104 | tf_op jit(solution)/shard_map/cond/branch_2_fun/ppermute | solution.py:158
  51.3 1.4 %collective-permute-start.17 = (bf16[4,16,1024]{2,1,0:T(8,128)(2,1)S(1)}, bf16[4,16,1024]{2,1,0:T(8,128)(2,1)}, u32[]{:S(2)}, u32[]{:S(2)}) collective-permute-start(bf16[4,16,1024]{2,1,0:T(8,128)(2,1)S(1)} %get-tuple-element.209), channel_id=1, source_target_pairs={{0,24},{8,16},{16,8},{24,0},{1,25},{9,17},{17,9},{25,1},{2,26},{10... | collective-permute-start | bytes 393224 | tf_op jit(solution)/shard_map/cond/branch_2_fun/ppermute | solution.py:158
  52.7 4.6 %collective-permute-done.17 = bf16[4,16,1024]{2,1,0:T(8,128)(2,1)} collective-permute-done((bf16[4,16,1024]{2,1,0:T(8,128)(2,1)S(1)}, bf16[4,16,1024]{2,1,0:T(8,128)(2,1)}, u32[]{:S(2)}, u32[]{:S(2)}) %collective-permute-start.17) | collective-permute-done | bytes 131104 | tf_op jit(solution)/shard_map/cond/branch_2_fun/ppermute | solution.py:158
  57.4 1.3 %collective-permute-done.13 = bf16[576,256]{1,0:T(8,128)(2,1)} collective-permute-done((bf16[576,256]{1,0:T(8,128)(2,1)S(1)}, bf16[576,256]{1,0:T(8,128)(2,1)}, u32[]{:S(2)}, u32[]{:S(2)}) %collective-permute-start.13) | collective-permute-done | bytes 294944 | tf_op jit(solution)/shard_map/cond/branch_2_fun/ppermute | solution.py:246
  58.7 1.1 %fusion.5 = (bf16[4,16,1024]{2,1,0:T(8,128)(2,1)S(1)}, f32[4,16,1024]{2,1,0:T(8,128)S(1)}) fusion(bf16[4,16,1024]{2,1,0:T(8,128)(2,1)} %get-tuple-element.336, bf16[4,16,1024]{2,1,0:T(8,128)(2,1)} %get-tuple-element.335, f32[4,16,1024]{2,1,0:T(8,128)S(1)} %get-tuple-element.310, bf16[4,16,1024]{2,1,0:T(8,128)(2,1)} %get-tuple-element.334), kind=kLoop, calls=%fused_computation.32 | loop fusion | flops 458752 | bytes 1048576 | tf_op jit(solution)/shard_map/convert_element_type | solution.py:300
  59.9 1.6 %collective-permute-start.96 = (bf16[16,1024]{1,0:T(8,128)(2,1)S(1)}, bf16[16,1024]{1,0:T(8,128)(2,1)S(1)}, u32[]{:S(2)}, u32[]{:S(2)}) collective-permute-start(bf16[16,1024]{1,0:T(8,128)(2,1)S(1)} %get-tuple-element.341), channel_id=1, source_target_pairs={{0,4},{1,5},{2,6},{3,7},{4,0},{5,1},{6,2},{7,3},{8,12},{9,13},{10,... | collective-permute-start | bytes 98312 | tf_op jit(solution)/shard_map/ppermute | solution.py:158
  61.5 2.8 %collective-permute-start.97 = (bf16[16,1024]{1,0:T(8,128)(2,1)S(1)}, bf16[16,1024]{1,0:T(8,128)(2,1)S(1)}, u32[]{:S(2)}, u32[]{:S(2)}) collective-permute-start(bf16[16,1024]{1,0:T(8,128)(2,1)S(1)} %get-tuple-element.340), channel_id=1, source_target_pairs={{0,6},{1,7},{2,4},{3,5},{4,2},{5,3},{6,0},{7,1},{8,14},{9,15},{10,... | collective-permute-start | bytes 98312 | tf_op jit(solution)/shard_map/ppermute | solution.py:158
  64.4 3.7 %weight_grads.1 = (bf16[384,1024]{1,0:T(8,128)(2,1)}, bf16[192,1024]{1,0:T(8,128)(2,1)}) custom-call(s32[8,1]{1,0:T(8,128)S(1)} %copy.12.relocate_ref, bf16[576,256]{1,0:T(8,128)(2,1)} %get-tuple-element.320.same_ref, bf16[576,256]{1,0:T(8,128)(2,1)} %get-tuple-element.321.cross_ref, bf16[256,2176]{1,0:T(8,128)(2,1)S(1)} %copy-done.5, ...), custom_call_target="tpu_custom_call" | custom-call | tf_op jit(solution)/shard_map/weight_grads/pallas_call | solution.py:304
  68.1 0.6 fusion.3
  (35 shorter events, 1.0 us)
Async XLA Ops:
  0.6 24.1 %copy-start = (bf16[1,1,384,1024]{3,2,1,0:T(8,128)(2,1)S(1)}, bf16[1,1,384,1024]{3,2,1,0:T(8,128)(2,1)}, u32[]{:S(2)}) copy-start(bf16[1,1,384,1024]{3,2,1,0:T(8,128)(2,1)} %param.26) | copy-start | bytes 2359300
  0.6 24.1 %copy-start.1 = (bf16[1,1,192,1024]{3,2,1,0:T(8,128)(2,1)S(1)}, bf16[1,1,192,1024]{3,2,1,0:T(8,128)(2,1)}, u32[]{:S(2)}) copy-start(bf16[1,1,192,1024]{3,2,1,0:T(8,128)(2,1)} %param.27) | copy-start | bytes 1179652
  2.3 0.8 %copy-start.2 = (bf16[16,1024]{1,0:T(8,128)(2,1)S(1)}, bf16[16,1024]{1,0:T(8,128)(2,1)}, u32[]{:S(2)}) copy-start(bf16[16,1024]{1,0:T(8,128)(2,1)} %tokens_ref.1) | copy-start | bytes 98308
  3.0 0.8 %copy-start.3 = (bf16[16,1024]{1,0:T(8,128)(2,1)S(1)}, bf16[16,1024]{1,0:T(8,128)(2,1)}, u32[]{:S(2)}) copy-start(bf16[16,1024]{1,0:T(8,128)(2,1)} %upstream_ref.1) | copy-start | bytes 98308
  3.9 9.5 %collective-permute-start.84 = (bf16[16,2176]{1,0:T(8,128)(2,1)S(1)}, bf16[16,2176]{1,0:T(8,128)(2,1)S(1)}, u32[]{:S(2)}, u32[]{:S(2)}) collective-permute-start(bf16[16,2176]{1,0:T(8,128)(2,1)S(1)} %pack.1), channel_id=1, source_target_pairs={{0,2},{1,3},{2,0},{3,1},{4,6},{5,7},{6,4},{7,5},{8,10},{9,11},{10,... | collective-permute-start | bytes 208904 | tf_op jit(solution)/shard_map/ppermute | solution.py:158
  7.0 8.0 %collective-permute-start.85 = (bf16[16,2176]{1,0:T(8,128)(2,1)S(1)}, bf16[16,2176]{1,0:T(8,128)(2,1)S(1)}, u32[]{:S(2)}, u32[]{:S(2)}) collective-permute-start(bf16[16,2176]{1,0:T(8,128)(2,1)S(1)} %pack.1), channel_id=1, source_target_pairs={{0,4},{1,5},{2,6},{3,7},{4,0},{5,1},{6,2},{7,3},{8,12},{9,13},{10,... | collective-permute-start | bytes 208904 | tf_op jit(solution)/shard_map/ppermute | solution.py:158
  9.6 6.2 %collective-permute-start.86 = (bf16[16,2176]{1,0:T(8,128)(2,1)S(1)}, bf16[16,2176]{1,0:T(8,128)(2,1)S(1)}, u32[]{:S(2)}, u32[]{:S(2)}) collective-permute-start(bf16[16,2176]{1,0:T(8,128)(2,1)S(1)} %pack.1), channel_id=1, source_target_pairs={{0,6},{1,7},{2,4},{3,5},{4,2},{5,3},{6,0},{7,1},{8,14},{9,15},{10,... | collective-permute-start | bytes 208904 | tf_op jit(solution)/shard_map/ppermute | solution.py:158
  9.6 6.2 %collective-permute-start.87 = (bf16[16,2176]{1,0:T(8,128)(2,1)S(1)}, bf16[16,2176]{1,0:T(8,128)(2,1)S(1)}, u32[]{:S(2)}, u32[]{:S(2)}) collective-permute-start(bf16[16,2176]{1,0:T(8,128)(2,1)S(1)} %pack.1), channel_id=1, source_target_pairs={{0,8},{8,0},{16,24},{24,16},{1,9},{9,1},{17,25},{25,17},{2,10},{10... | collective-permute-start | bytes 208904 | tf_op jit(solution)/shard_map/ppermute | solution.py:158
  11.3 5.1 %collective-permute-start.88 = (bf16[16,2176]{1,0:T(8,128)(2,1)S(1)}, bf16[16,2176]{1,0:T(8,128)(2,1)S(1)}, u32[]{:S(2)}, u32[]{:S(2)}) collective-permute-start(bf16[16,2176]{1,0:T(8,128)(2,1)S(1)} %pack.1), channel_id=1, source_target_pairs={{0,16},{8,24},{16,0},{24,8},{1,17},{9,25},{17,1},{25,9},{2,18},{10... | collective-permute-start | bytes 208904 | tf_op jit(solution)/shard_map/ppermute | solution.py:158
  13.4 5.2 %collective-permute-start.89 = (bf16[16,2176]{1,0:T(8,128)(2,1)S(1)}, bf16[16,2176]{1,0:T(8,128)(2,1)S(1)}, u32[]{:S(2)}, u32[]{:S(2)}) collective-permute-start(bf16[16,2176]{1,0:T(8,128)(2,1)S(1)} %pack.1), channel_id=1, source_target_pairs={{0,24},{8,16},{16,8},{24,0},{1,25},{9,17},{17,9},{25,1},{2,26},{10... | collective-permute-start | bytes 208904 | tf_op jit(solution)/shard_map/ppermute | solution.py:158
  21.2 6.8 %collective-permute-start.90 = (bf16[48,2176]{1,0:T(8,128)(2,1)S(1)}, bf16[48,2176]{1,0:T(8,128)(2,1)S(1)}, u32[]{:S(2)}, u32[]{:S(2)}) collective-permute-start(bf16[48,2176]{1,0:T(8,128)(2,1)S(1)} %constant_dynamic-update-slice_fusion), channel_id=1, source_target_pairs={{0,8},{8,0},{16,24},{24,16},{1,9},{9,1},{17,25},{25,17},{2,10},{10... | collective-permute-start | bytes 626696 | tf_op jit(solution)/shard_map/ppermute | solution.py:158
  21.8 9.4 %collective-permute-start.91 = (bf16[48,2176]{1,0:T(8,128)(2,1)S(1)}, bf16[48,2176]{1,0:T(8,128)(2,1)S(1)}, u32[]{:S(2)}, u32[]{:S(2)}) collective-permute-start(bf16[48,2176]{1,0:T(8,128)(2,1)S(1)} %constant_dynamic-update-slice_fusion), channel_id=1, source_target_pairs={{0,16},{8,24},{16,0},{24,8},{1,17},{9,25},{17,1},{25,9},{2,18},{10... | collective-permute-start | bytes 626696 | tf_op jit(solution)/shard_map/ppermute | solution.py:158
  22.1 9.7 %collective-permute-start.92 = (bf16[48,2176]{1,0:T(8,128)(2,1)S(1)}, bf16[48,2176]{1,0:T(8,128)(2,1)S(1)}, u32[]{:S(2)}, u32[]{:S(2)}) collective-permute-start(bf16[48,2176]{1,0:T(8,128)(2,1)S(1)} %constant_dynamic-update-slice_fusion), channel_id=1, source_target_pairs={{0,24},{8,16},{16,8},{24,0},{1,25},{9,17},{17,9},{25,1},{2,26},{10... | collective-permute-start | bytes 626696 | tf_op jit(solution)/shard_map/ppermute | solution.py:158
  24.7 12.7 %collective-permute-start.93 = (bf16[384,1024]{1,0:T(8,128)(2,1)S(1)}, bf16[384,1024]{1,0:T(8,128)(2,1)S(1)}, u32[]{:S(2)}, u32[]{:S(2)}) collective-permute-start(bf16[384,1024]{1,0:T(8,128)(2,1)S(1)} %bitcast.24), channel_id=1, source_target_pairs={{0,1},{1,0},{2,3},{3,2},{4,5},{5,4},{6,7},{7,6},{8,9},{9,8},{10,11... | collective-permute-start | bytes 2359304 | tf_op jit(solution)/shard_map/ppermute | solution.py:158
  24.7 12.7 %collective-permute-start.94 = (bf16[192,1024]{1,0:T(8,128)(2,1)S(1)}, bf16[192,1024]{1,0:T(8,128)(2,1)S(1)}, u32[]{:S(2)}, u32[]{:S(2)}) collective-permute-start(bf16[192,1024]{1,0:T(8,128)(2,1)S(1)} %bitcast.26), channel_id=1, source_target_pairs={{0,1},{1,0},{2,3},{3,2},{4,5},{5,4},{6,7},{7,6},{8,9},{9,8},{10,11... | collective-permute-start | bytes 1179656 | tf_op jit(solution)/shard_map/ppermute | solution.py:158
  37.5 3.1 %copy-start.4 = (bf16[256,2176]{1,0:T(8,128)(2,1)S(1)}, bf16[256,2176]{1,0:T(8,128)(2,1)}, u32[]{:S(2)}) copy-start(bf16[256,2176]{1,0:T(8,128)(2,1)} %slice_dynamic-update-slice_fusion.plane_ref) | copy-start | bytes 3342340
  40.5 23.8 %copy-start.6 = (s32[8,1]{0,1:T(1,128)S(1)}, s32[8,1]{0,1:T(1,128)}, u32[]{:S(2)}) copy-start(s32[8,1]{0,1:T(1,128)} %param.25) | copy-start | bytes 100
  40.5 23.9 %copy-start.5 = (bf16[256,2176]{1,0:T(8,128)(2,1)S(1)}, bf16[256,2176]{1,0:T(8,128)(2,1)}, u32[]{:S(2)}) copy-start(bf16[256,2176]{1,0:T(8,128)(2,1)} %slice_dynamic-update-slice_fusion.plane_ref) | copy-start | bytes 3342340
  40.6 18.1 %collective-permute-start.14 = (bf16[256,2176]{1,0:T(8,128)(2,1)S(1)}, bf16[256,2176]{1,0:T(8,128)(2,1)}, u32[]{:S(2)}, u32[]{:S(2)}) collective-permute-start(bf16[256,2176]{1,0:T(8,128)(2,1)S(1)} %get-tuple-element.206), channel_id=1, source_target_pairs={{0,1},{1,0},{2,3},{3,2},{4,5},{5,4},{6,7},{7,6},{8,9},{9,8},{10,11... | collective-permute-start | bytes 3342344 | tf_op jit(solution)/shard_map/cond/branch_2_fun/ppermute | solution.py:158
  40.6 16.7 %collective-permute-start.12 = (bf16[576,256]{1,0:T(8,128)(2,1)S(1)}, bf16[576,256]{1,0:T(8,128)(2,1)}, u32[]{:S(2)}, u32[]{:S(2)}) collective-permute-start(bf16[576,256]{1,0:T(8,128)(2,1)S(1)} %get-tuple-element.204), channel_id=1, source_target_pairs={{0,4},{1,5},{2,2},{3,3},{4,0},{5,1},{6,6},{7,7},{8,12},{9,13},{10,... | collective-permute-start | bytes 884744 | tf_op jit(solution)/shard_map/cond/branch_2_fun/ppermute | solution.py:243
  44.2 14.5 %collective-permute-start.13 = (bf16[576,256]{1,0:T(8,128)(2,1)S(1)}, bf16[576,256]{1,0:T(8,128)(2,1)}, u32[]{:S(2)}, u32[]{:S(2)}) collective-permute-start(bf16[576,256]{1,0:T(8,128)(2,1)S(1)} %get-tuple-element.205), channel_id=1, source_target_pairs={{0,5},{1,4},{2,3},{3,2},{4,1},{5,0},{6,7},{7,6},{8,13},{9,12},{10,... | collective-permute-start | bytes 884744 | tf_op jit(solution)/shard_map/cond/branch_2_fun/ppermute | solution.py:246
  45.4 5.9 %collective-permute-start.15 = (bf16[4,16,1024]{2,1,0:T(8,128)(2,1)S(1)}, bf16[4,16,1024]{2,1,0:T(8,128)(2,1)}, u32[]{:S(2)}, u32[]{:S(2)}) collective-permute-start(bf16[4,16,1024]{2,1,0:T(8,128)(2,1)S(1)} %get-tuple-element.207), channel_id=1, source_target_pairs={{0,8},{8,0},{16,24},{24,16},{1,9},{9,1},{17,25},{25,17},{2,10},{10... | collective-permute-start | bytes 393224 | tf_op jit(solution)/shard_map/cond/branch_2_fun/ppermute | solution.py:158
  46.4 6.4 %collective-permute-start.16 = (bf16[4,16,1024]{2,1,0:T(8,128)(2,1)S(1)}, bf16[4,16,1024]{2,1,0:T(8,128)(2,1)}, u32[]{:S(2)}, u32[]{:S(2)}) collective-permute-start(bf16[4,16,1024]{2,1,0:T(8,128)(2,1)S(1)} %get-tuple-element.208), channel_id=1, source_target_pairs={{0,16},{8,24},{16,0},{24,8},{1,17},{9,25},{17,1},{25,9},{2,18},{10... | collective-permute-start | bytes 393224 | tf_op jit(solution)/shard_map/cond/branch_2_fun/ppermute | solution.py:158
  51.3 6.1 %collective-permute-start.17 = (bf16[4,16,1024]{2,1,0:T(8,128)(2,1)S(1)}, bf16[4,16,1024]{2,1,0:T(8,128)(2,1)}, u32[]{:S(2)}, u32[]{:S(2)}) collective-permute-start(bf16[4,16,1024]{2,1,0:T(8,128)(2,1)S(1)} %get-tuple-element.209), channel_id=1, source_target_pairs={{0,24},{8,16},{16,8},{24,0},{1,25},{9,17},{17,9},{25,1},{2,26},{10... | collective-permute-start | bytes 393224 | tf_op jit(solution)/shard_map/cond/branch_2_fun/ppermute | solution.py:158
  59.8 8.3 %collective-permute-start.95 = (bf16[16,1024]{1,0:T(8,128)(2,1)S(1)}, bf16[16,1024]{1,0:T(8,128)(2,1)S(1)}, u32[]{:S(2)}, u32[]{:S(2)}) collective-permute-start(bf16[16,1024]{1,0:T(8,128)(2,1)S(1)} %get-tuple-element.339), channel_id=1, source_target_pairs={{0,2},{1,3},{2,0},{3,1},{4,6},{5,7},{6,4},{7,5},{8,10},{9,11},{10,... | collective-permute-start | bytes 98312 | tf_op jit(solution)/shard_map/ppermute | solution.py:158
  59.9 8.2 %collective-permute-start.96 = (bf16[16,1024]{1,0:T(8,128)(2,1)S(1)}, bf16[16,1024]{1,0:T(8,128)(2,1)S(1)}, u32[]{:S(2)}, u32[]{:S(2)}) collective-permute-start(bf16[16,1024]{1,0:T(8,128)(2,1)S(1)} %get-tuple-element.341), channel_id=1, source_target_pairs={{0,4},{1,5},{2,6},{3,7},{4,0},{5,1},{6,2},{7,3},{8,12},{9,13},{10,... | collective-permute-start | bytes 98312 | tf_op jit(solution)/shard_map/ppermute | solution.py:158
  61.5 6.6 %collective-permute-start.97 = (bf16[16,1024]{1,0:T(8,128)(2,1)S(1)}, bf16[16,1024]{1,0:T(8,128)(2,1)S(1)}, u32[]{:S(2)}, u32[]{:S(2)}) collective-permute-start(bf16[16,1024]{1,0:T(8,128)(2,1)S(1)} %get-tuple-element.340), channel_id=1, source_target_pairs={{0,6},{1,7},{2,4},{3,5},{4,2},{5,3},{6,0},{7,1},{8,14},{9,15},{10,... | collective-permute-start | bytes 98312 | tf_op jit(solution)/shard_map/ppermute | solution.py:158

commit v2 on v1

--- a/solution.py
+++ b/solution.py
@@ -162,26 +162,34 @@
     return [pl.BlockSpec(memory_space=pltpu.VMEM)] * count
 
 
-def pack_kernel(n_cols, ids_ref, gates_ref, tokens_ref, upstream_ref, packed_ref):
-    width = tokens_ref.shape[1]
-    lane = lax.broadcasted_iota(jnp.int32, (tokens_ref.shape[0], 128), 1)
-    table = jnp.zeros(lane.shape, jnp.float32)
-    for k in range(ids_ref.shape[1]):
-        table += jnp.where(ids_ref[:, k : k + 1] == lane % n_cols, gates_ref[:, k : k + 1], 0.0)
-    high = table.astype(jnp.bfloat16)
-    rest = table - high.astype(jnp.float32)
-    middle = rest.astype(jnp.bfloat16)
-    low = (rest - middle.astype(jnp.float32)).astype(jnp.bfloat16)
-    zero = jnp.zeros_like(high)
-    part = lane // n_cols
-    packed_ref[:, :width] = tokens_ref[...]
-    packed_ref[:, width : 2 * width] = upstream_ref[...]
-    packed_ref[:, 2 * width :] = jnp.where(
-        part == 0, high, jnp.where(part == 1, middle, jnp.where(part == 2, low, zero))
-    )
-
-
-def forward_kernel(n_cols, n_rows, tok_dev, plane_ref, wgu_own, wdn_own, wgu_sib, wdn_sib, own_ref, sib_ref, kept_ref, *sent_refs):
+def packed(tokens, upstream, expert_ids, gates, n_cols):
+    tok_dev, width = tokens.shape
+    column = jnp.arange(128, dtype=jnp.int32)[None, :]
+    table = jnp.zeros((tok_dev, 128), jnp.float32)
+    for k in range(expert_ids.shape[1]):
+        table = table + jnp.where(expert_ids[:, k : k + 1] == column % n_cols, gates[:, k : k + 1], 0.0)
+    high = lax.reduce_precision(table, 8, 7)
+    middle = lax.reduce_precision(table - high, 8, 7)
+    part = column // n_cols
+    table = jnp.where(part == 0, high, jnp.where(part == 1, middle, jnp.where(part == 2, table - high - middle, 0.0)))
+    return jnp.concatenate([tokens, upstream, table.astype(jnp.bfloat16)], axis=1)
+
+
+def forward_kernel(n_cols, n_rows, n_z, *refs):
+    near = refs[: n_rows + n_z - 1]
+    far = refs[n_rows + n_z - 1 : 2 * n_rows + n_z - 2]
+    wgu_own, wdn_own, wgu_sib, wdn_sib, plane_ref, own_ref, sib_ref, kept_ref, *sent_refs = refs[2 * n_rows + n_z - 2 :]
+    tok_dev = near[0].shape[0]
+    for z in range(n_z):
+        for d in range(n_rows):
+            start = (z * n_rows + d) * tok_dev
+            if z == 0:
+                block = near[d][...]
+            elif d == 0:
+                block = near[n_rows + z - 1][...]
+            else:
+                block = far[d - 1][(z - 1) * tok_dev : z * tok_dev]
+            plane_ref[start : start + tok_dev] = block
     units, width = wdn_own.shape
     col_here = lax.axis_index("expert")
     lane = lax.broadcasted_iota(jnp.int32, (8, 128), 1)
@@ -205,7 +213,7 @@
         acts_ref[2 * units :] = (activated * up_pre * gate).astype(jnp.bfloat16)
         part = lax.dot_general(acts_ref[: 2 * units], wgu[...], contract_first, preferred_element_type=jnp.float32)
         total = part if total is None else total + part
-    for z in range(plane_ref.shape[0] // (n_rows * tok_dev)):
+    for z in range(n_z):
         for d in range(n_rows):
             start = (z * n_rows + d) * tok_dev
             block = total[start : start + tok_dev]
@@ -215,22 +223,22 @@
                 sent_refs[d - 1][z] = block.astype(jnp.bfloat16)
 
 
+def halves_swapped(acts):
+    half = acts.shape[1] // 2
+    return jnp.concatenate([acts[:, half:], acts[:, :half]], axis=1)
+
+
 def weight_grad_kernel(relocate_ref, same_ref, cross_ref, plane_ref, other_ref, gu_ref, dn_ref):
     units, width = dn_ref.shape
-    half = plane_ref.shape[0] // 2
-    first = pl.multiple_of(relocate_ref[lax.axis_index("expert"), 0] * half, half)
-    for acts, rows_ref, start in ((same_ref, plane_ref, True), (cross_ref, other_ref, False)):
-        for side in range(2):
-            rows = pl.ds(first if side == 0 else half - first, half)
-            lanes = slice(side * half, (side + 1) * half)
-            gu = jnp.dot(acts[: 2 * units, lanes], rows_ref[rows, :width], preferred_element_type=jnp.float32)
-            dn = jnp.dot(acts[2 * units :, lanes], rows_ref[rows, width : 2 * width], preferred_element_type=jnp.float32)
-            if start and side == 0:
-                gu_sum, dn_sum = gu, dn
-            else:
-                gu_sum, dn_sum = gu_sum + gu, dn_sum + dn
-    gu_ref[...] = gu_sum.astype(jnp.bfloat16)
-    dn_ref[...] = dn_sum.astype(jnp.bfloat16)
+    moved = relocate_ref[lax.axis_index("expert"), 0] == 1
+    same = jnp.where(moved, halves_swapped(same_ref[...]), same_ref[...])
+    cross = jnp.where(moved, halves_swapped(cross_ref[...]), cross_ref[...])
+    for out, low, start in ((gu_ref, 0, 0), (dn_ref, 2 * units, width)):
+        high = low + out.shape[0]
+        out[...] = (
+            jnp.dot(same[low:high], plane_ref[:, start : start + width], preferred_element_type=jnp.float32)
+            + jnp.dot(cross[low:high], other_ref[:, start : start + width], preferred_element_type=jnp.float32)
+        ).astype(jnp.bfloat16)
 
 
 def exchanges(pattern, acts_own, acts_sib, plane, sent_rows):
@@ -242,8 +250,10 @@
 
     got_same = lax.ppermute(acts_own, "expert", [(col, place(col)) for col in range(n_cols)])
     got = [crossed(block, "dp", d + 1) for d, block in enumerate(sent_rows)]
+    got_same, acts_sib = lax.optimization_barrier((got_same, acts_sib))
+    got_cross = lax.ppermute(acts_sib, "expert", [(col, place(col ^ 1)) for col in range(n_cols)])
+    got_same, got, plane = lax.optimization_barrier((got_same, got, plane))
     plane_sib = crossed(plane, "expert", 1)
-    got_cross = lax.ppermute(acts_sib, "expert", [(col, place(col ^ 1)) for col in range(n_cols)])
     return got_same, got_cross, plane_sib, got
 
 
@@ -255,17 +265,10 @@
     half = n_cols // 2
     units, width = w_down.shape[2:]
     plane_rows = n_rows * n_z * tok_dev
-    limit = pltpu.CompilerParams(vmem_limit_bytes=48 * 2**20)
+    limit = pltpu.CompilerParams(vmem_limit_bytes=16 * 2**20)
     bf16 = jnp.bfloat16
 
-    own = pl.pallas_call(
-        functools.partial(pack_kernel, n_cols),
-        out_shape=jax.ShapeDtypeStruct((tok_dev, 2 * width + 128), bf16),
-        in_specs=whole(4),
-        out_specs=whole(1)[0],
-        compiler_params=limit,
-        name="pack",
-    )(expert_ids, gates, tokens, upstream)
+    own = packed(tokens, upstream, expert_ids, gates, n_cols)
 
     along_dp = [crossed(own, "dp", d) for d in range(1, n_rows)]
     along_z = [crossed(own, "expert", 2 * dz) for dz in range(1, n_z)]
@@ -276,21 +279,16 @@
     wgu_own, wdn_own = w_gate_up[0, 0], w_down[0, 0]
     wgu_sib = crossed(wgu_own, "expert", 1)
     wdn_sib = crossed(wdn_own, "expert", 1)
-    plane = [own] + along_dp
-    for dz in range(n_z - 1):
-        plane += [along_z[dz]] + [block[dz * tok_dev : (dz + 1) * tok_dev] for block in far_dp]
-    plane = jnp.concatenate(plane, axis=0)
-
     acts = jax.ShapeDtypeStruct((3 * units, plane_rows), bf16)
-    acts_own, acts_sib, kept, *sent = pl.pallas_call(
-        functools.partial(forward_kernel, n_cols, n_rows, tok_dev),
-        out_shape=[acts, acts, jax.ShapeDtypeStruct((n_z, tok_dev, width), jnp.float32)]
+    plane, acts_own, acts_sib, kept, *sent = pl.pallas_call(
+        functools.partial(forward_kernel, n_cols, n_rows, n_z),
+        out_shape=[jax.ShapeDtypeStruct((plane_rows, own.shape[1]), bf16), acts, acts, jax.ShapeDtypeStruct((n_z, tok_dev, width), jnp.float32)]
         + [jax.ShapeDtypeStruct((n_z, tok_dev, width), bf16)] * (n_rows - 1),
-        in_specs=whole(5),
-        out_specs=whole(2 + n_rows),
+        in_specs=whole(2 * n_rows + n_z + 2),
+        out_specs=whole(3 + n_rows),
         compiler_params=limit,
         name="forward",
-    )(plane, wgu_own, wdn_own, wgu_sib, wdn_sib)
+    )(own, *along_dp, *along_z, *far_dp, wgu_own, wdn_own, wgu_sib, wdn_sib)
 
     branches = [functools.partial(exchanges, pattern) for pattern in range(1, (1 << half) - 1)]
     got_same, got_cross, plane_sib, got = lax.switch(bits - 1, branches, acts_own, acts_sib, plane, sent)

time: 68.5 us -> 67.5 us (0.985); the launches traced: 68.8 us -> 66.6 us
  local copies, waits for them, and re-layouts: 13.3 us -> 5.22 us
  waiting for transfers between devices: 18.2 us -> 25.9 us
  Pallas kernels: 6.87 us -> 4.75 us
  other arithmetic: 3.02 us -> 4.01 us
    unnamed x33 -> x13, local copies, waits for them, and re-layouts: 12.7 us -> 3.23 us
    ppermute x1, waiting for transfers between devices: 1.33 us -> 9.87 us  [exchanges(): lax.ppermute(acts_sib, 'expert', [(col, place(col ^ 1)) for col in range(...]
    ppermute x18, waiting for transfers between devices: 16.9 us -> 11.4 us  [crossed(): lax.ppermute(block, axis, [(i, i ^ apart) for i in range(lax.axis_size(ax...]
    ppermute x1, waiting for transfers between devices: 0.01 us -> 4.59 us  [exchanges(): lax.ppermute(acts_own, 'expert', [(col, place(col)) for col in range(n_co...]
    pallas_call x2 -> x1, Pallas kernels: 3.14 us -> 1.72 us  [dense_device(): pl.pallas_call(functools.partial(forward_kernel, n_cols, n_rows, n_z), ou...]
    eq x0 -> x1, local copies, waits for them, and re-layouts: none -> 0.99 us  [packed(): expert_ids[:, k:k + 1] == column % n_cols]
    broadcast_in_dim x0 -> x1, local copies, waits for them, and re-layouts: none -> 0.98 us  [packed(): jnp.where(expert_ids[:, k:k + 1] == column % n_cols, gates[:, k:k + 1], 0.0)]
    concatenate x0 -> x1, other arithmetic: none -> 0.78 us  [packed(): jnp.concatenate([tokens, upstream, table.astype(jnp.bfloat16)], axis=1)]
  transfers between devices with their start and end apart: 20 -> 20, of which waited for: 8 -> 8; matrix products, arithmetic and copies ran while one was open for 13% -> 2% of each run, Pallas kernels for 5% -> 5%
where the time goes in v2:
time: 67.5 us; the launch traced here: 66.6 us
  waiting for transfers between devices  25.9 us (38%)
  starting transfers between devices  25.3 us (37%)
  local copies, waits for them, and re-layouts  5.22 us (8%)
  Pallas kernels  4.75 us (7%)
  other arithmetic  4.01 us (6%)
  between operations  1.41 us (2%)
    ppermute x18, starting transfers between devices, crossed(): lax.ppermute(block, axis, [(i, i ^ apart) for i in range(lax.axis_size(ax...  21.2 us
    ppermute x18, waiting for transfers between devices, crossed(): lax.ppermute(block, axis, [(i, i ^ apart) for i in range(lax.axis_size(ax...  11.4 us
    ppermute x1, waiting for transfers between devices, exchanges(): lax.ppermute(acts_sib, 'expert', [(col, place(col ^ 1)) for col in range(...  9.87 us
    ppermute x1, waiting for transfers between devices, exchanges(): lax.ppermute(acts_own, 'expert', [(col, place(col)) for col in range(n_co...  4.59 us
    ppermute x1, starting transfers between devices, exchanges(): lax.ppermute(acts_own, 'expert', [(col, place(col)) for col in range(n_co...  3.59 us
    unnamed x13, local copies, waits for them, and re-layouts  3.23 us
    pallas_call x1, Pallas kernels, dense_device(): pl.pallas_call(weight_grad_kernel, out_shape=[jax.ShapeDtypeStruct((2 * u...  3.03 us
    pallas_call x1, Pallas kernels, dense_device(): pl.pallas_call(functools.partial(forward_kernel, n_cols, n_rows, n_z), ou...  1.72 us
  transfers between devices with their start and end apart: 20, of which 8 were waited for; matrix products, arithmetic and copies ran while one was open for 2% of the time, Pallas kernels for 5%

profile of v2, /device:TPU:0, one launch (start us, length us, event | category | flops | bytes accessed | tf_op | source)
XLA Modules:
  0.0 66.6 jit_solution(3595387825718198025)
XLA Ops:
  0.7 1.0 %slice_bitcast_fusion.19 = (s32[16]{0:T(128)S(1)}, s32[16]{0:T(128)S(1)}, s32[16]{0:T(128)S(1)}, s32[16]{0:T(128)S(1)}, s32[16]{0:T(128)S(1)}, /*index=5*/s32[16]{0:T(128)S(1)}, s32[16]{0:T(128)S(1)}, s32[16]{0:T(128)S(1)}) fusion(s32[16,8]{0,1:T(8,128)} %param.23), kind=kLoop, calls=%fused_computation.41 | loop fusion | bytes 1024 | tf_op jit(solution)/shard_map/eq | solution.py:170
  1.7 1.0 %slice_bitcast_fusion.18 = (f32[16]{0:T(128)S(1)}, f32[16]{0:T(128)S(1)}, f32[16]{0:T(128)S(1)}, f32[16]{0:T(128)S(1)}, f32[16]{0:T(128)S(1)}, /*index=5*/f32[16]{0:T(128)S(1)}, f32[16]{0:T(128)S(1)}, f32[16]{0:T(128)S(1)}) fusion(f32[16,8]{0,1:T(8,128)} %param.24), kind=kLoop, calls=%fused_computation.40 | loop fusion | bytes 1024 | tf_op jit(solution)/shard_map/jit(_where)/broadcast_in_dim | solution.py:170
  2.6 0.1 fusion.4
  2.7 0.8 %pad_maximum_fusion.refs_0_ = bf16[16,2176]{1,0:T(8,128)(2,1)S(1)} fusion(bf16[16,128]{1,0:T(8,128)(2,1)S(1)} %fusion.4, bf16[16,1024]{1,0:T(8,128)(2,1)} %param.22, bf16[16,1024]{1,0:T(8,128)(2,1)} %param.21), kind=kLoop, calls=%fused_computation.1 | loop fusion | flops 208896 | bytes 139264 | tf_op jit(solution)/shard_map/concatenate | solution.py:175
  3.5 3.0 %collective-permute-start.84 = (bf16[16,2176]{1,0:T(8,128)(2,1)S(1)}, bf16[16,2176]{1,0:T(8,128)(2,1)S(1)}, u32[]{:S(2)}, u32[]{:S(2)}) collective-permute-start(bf16[16,2176]{1,0:T(8,128)(2,1)S(1)} %pad_maximum_fusion.refs_0_), channel_id=1, source_target_pairs={{0,2},{1,3},{2,0},{3,1},{4,6},{5,7},{6,4},{7,5},{8,10},{9,11},{10,... | collective-permute-start | bytes 208904 | tf_op jit(solution)/shard_map/ppermute | solution.py:158
  6.5 2.6 %collective-permute-start.85 = (bf16[16,2176]{1,0:T(8,128)(2,1)S(1)}, bf16[16,2176]{1,0:T(8,128)(2,1)S(1)}, u32[]{:S(2)}, u32[]{:S(2)}) collective-permute-start(bf16[16,2176]{1,0:T(8,128)(2,1)S(1)} %pad_maximum_fusion.refs_0_), channel_id=1, source_target_pairs={{0,4},{1,5},{2,6},{3,7},{4,0},{5,1},{6,2},{7,3},{8,12},{9,13},{10,... | collective-permute-start | bytes 208904 | tf_op jit(solution)/shard_map/ppermute | solution.py:158
  9.1 0.0 collective-permute-start.86
  9.1 1.7 %collective-permute-start.87 = (bf16[16,2176]{1,0:T(8,128)(2,1)S(1)}, bf16[16,2176]{1,0:T(8,128)(2,1)S(1)}, u32[]{:S(2)}, u32[]{:S(2)}) collective-permute-start(bf16[16,2176]{1,0:T(8,128)(2,1)S(1)} %pad_maximum_fusion.refs_0_), channel_id=1, source_target_pairs={{0,8},{8,0},{16,24},{24,16},{1,9},{9,1},{17,25},{25,17},{2,10},{10... | collective-permute-start | bytes 208904 | tf_op jit(solution)/shard_map/ppermute | solution.py:158
  10.9 1.5 %collective-permute-start.88 = (bf16[16,2176]{1,0:T(8,128)(2,1)S(1)}, bf16[16,2176]{1,0:T(8,128)(2,1)S(1)}, u32[]{:S(2)}, u32[]{:S(2)}) collective-permute-start(bf16[16,2176]{1,0:T(8,128)(2,1)S(1)} %pad_maximum_fusion.refs_0_), channel_id=1, source_target_pairs={{0,16},{8,24},{16,0},{24,8},{1,17},{9,25},{17,1},{25,9},{2,18},{10... | collective-permute-start | bytes 208904 | tf_op jit(solution)/shard_map/ppermute | solution.py:158
  12.4 0.3 collective-permute-start.89
  12.6 1.3 %fusion.6 = s32[]{:T(128)} fusion(s32[8,1]{0,1:T(1,128)} %param.25), kind=kLoop, calls=%fused_computation.25 | loop fusion | flops 7 | bytes 20 | tf_op jit(solution)/shard_map/reduce_sum | solution.py:275
  13.9 0.1 collective-permute-done.85.refs_5_
  14.1 1.3 %collective-permute-done.86.refs_6_ = bf16[16,2176]{1,0:T(8,128)(2,1)S(1)} collective-permute-done((bf16[16,2176]{1,0:T(8,128)(2,1)S(1)}, bf16[16,2176]{1,0:T(8,128)(2,1)S(1)}, u32[]{:S(2)}, u32[]{:S(2)}) %collective-permute-start.86) | collective-permute-done | bytes 69664 | tf_op jit(solution)/shard_map/ppermute | solution.py:158
  15.4 0.0 collective-permute-done.87.refs_1_
  15.4 0.5 collective-permute-done.88.refs_2_
  15.9 1.7 %collective-permute-done.89.refs_3_ = bf16[16,2176]{1,0:T(8,128)(2,1)S(1)} collective-permute-done((bf16[16,2176]{1,0:T(8,128)(2,1)S(1)}, bf16[16,2176]{1,0:T(8,128)(2,1)S(1)}, u32[]{:S(2)}, u32[]{:S(2)}) %collective-permute-start.89) | collective-permute-done | bytes 69664 | tf_op jit(solution)/shard_map/ppermute | solution.py:158
  17.6 0.0 collective-permute-start.93
  17.6 0.5 collective-permute-start.94
  18.1 0.6 collective-permute-start.90
  18.7 0.3 collective-permute-start.91
  19.1 2.6 %collective-permute-start.92 = (bf16[48,2176]{1,0:T(8,128)(2,1)S(1)}, bf16[48,2176]{1,0:T(8,128)(2,1)S(1)}, u32[]{:S(2)}, u32[]{:S(2)}) collective-permute-start(bf16[48,2176]{1,0:T(8,128)(2,1)S(1)} %constant_dynamic-update-slice_fusion), channel_id=1, source_target_pairs={{0,24},{8,16},{16,8},{24,0},{1,25},{9,17},{17,9},{25,1},{2,26},{10... | collective-permute-start | bytes 626696 | tf_op jit(solution)/shard_map/ppermute | solution.py:158
  22.3 3.9 %collective-permute-done.90.refs_7_ = bf16[48,2176]{1,0:T(8,128)(2,1)S(1)} collective-permute-done((bf16[48,2176]{1,0:T(8,128)(2,1)S(1)}, bf16[48,2176]{1,0:T(8,128)(2,1)S(1)}, u32[]{:S(2)}, u32[]{:S(2)}) %collective-permute-start.90) | collective-permute-done | bytes 208928 | tf_op jit(solution)/shard_map/ppermute | solution.py:158
  26.2 3.9 %collective-permute-done.91.refs_8_ = bf16[48,2176]{1,0:T(8,128)(2,1)S(1)} collective-permute-done((bf16[48,2176]{1,0:T(8,128)(2,1)S(1)}, bf16[48,2176]{1,0:T(8,128)(2,1)S(1)}, u32[]{:S(2)}, u32[]{:S(2)}) %collective-permute-start.91) | collective-permute-done | bytes 208928 | tf_op jit(solution)/shard_map/ppermute | solution.py:158
  30.1 0.0 collective-permute-done.94.refs_13_
  30.1 0.0 collective-permute-done.93.refs_12_
  30.1 0.0 copy-start
  30.1 1.1 %copy-done = bf16[1,1,384,1024]{3,2,1,0:T(8,128)(2,1)S(1)} copy-done((bf16[1,1,384,1024]{3,2,1,0:T(8,128)(2,1)S(1)}, bf16[1,1,384,1024]{3,2,1,0:T(8,128)(2,1)}, u32[]{:S(2)}) %copy-start) | copy-done | bytes 786456
  31.2 1.0 %copy-done.1 = bf16[1,1,192,1024]{3,2,1,0:T(8,128)(2,1)S(1)} copy-done((bf16[1,1,192,1024]{3,2,1,0:T(8,128)(2,1)S(1)}, bf16[1,1,192,1024]{3,2,1,0:T(8,128)(2,1)}, u32[]{:S(2)}) %copy-start.1) | copy-done | bytes 393240
  32.2 1.7 %forward.1 = (bf16[256,2176]{1,0:T(8,128)(2,1)S(1)}, bf16[576,256]{1,0:T(8,128)(2,1)S(1)}, bf16[576,256]{1,0:T(8,128)(2,1)S(1)}, f32[4,16,1024]{2,1,0:T(8,128)S(...) custom-call(bf16[16,2176]{1,0:T(8,128)(2,1)S(1)} %pad_maximum_fusion.refs_0, ...), custom_call_target="tpu_custom_call" | custom-call | tf_op jit(solution)/shard_map/forward/pallas_call | solution.py:283
  33.9 0.0 copy-start.4
  34.0 1.0 %copy-done.2 = bf16[256,2176]{1,0:T(8,128)(2,1)} copy-done((bf16[256,2176]{1,0:T(8,128)(2,1)}, bf16[256,2176]{1,0:T(8,128)(2,1)S(1)}, u32[]{:S(2)}) %copy-start.2) | copy-done | bytes 1114136
  35.0 22.2 %conditional.1 = (bf16[576,256]{1,0:T(8,128)(2,1)}, bf16[576,256]{1,0:T(8,128)(2,1)}, bf16[256,2176]{1,0:T(8,128)(2,1)}, bf16[4,16,1024]{2,1,0:T(8,128)(2,1)}, b...) conditional(s32[]{:T(128)} %clamp.3, (bf16[576,256]{1,0:T(8,128)(2,1)S(1)}, ...), branch_computations={%region_1.2_spmd, %region_2.3_spmd, %region_3.4_spmd, %region_4.5_... | conditional | bytes 8388896 | solution.py:294
  35.0 3.6 %collective-permute-start.48 = (bf16[576,256]{1,0:T(8,128)(2,1)S(1)}, bf16[576,256]{1,0:T(8,128)(2,1)}, u32[]{:S(2)}, u32[]{:S(2)}) collective-permute-start(bf16[576,256]{1,0:T(8,128)(2,1)S(1)} %get-tuple-element.272), channel_id=1, source_target_pairs={{0,4},{1,1},{2,2},{3,7},{4,0},{5,5},{6,6},{7,3},{8,12},{9,9},{10,1... | collective-permute-start | bytes 884744 | tf_op jit(solution)/shard_map/cond/branch_8_fun/ppermute | solution.py:251
  38.6 1.6 %collective-permute-start.49 = (bf16[4,16,1024]{2,1,0:T(8,128)(2,1)S(1)}, bf16[4,16,1024]{2,1,0:T(8,128)(2,1)}, u32[]{:S(2)}, u32[]{:S(2)}) collective-permute-start(bf16[4,16,1024]{2,1,0:T(8,128)(2,1)S(1)} %get-tuple-element.275), channel_id=1, source_target_pairs={{0,8},{8,0},{16,24},{24,16},{1,9},{9,1},{17,25},{25,17},{2,10},{10... | collective-permute-start | bytes 393224 | tf_op jit(solution)/shard_map/cond/branch_8_fun/ppermute | solution.py:158
  40.1 0.5 collective-permute-start.50
  40.6 1.5 %collective-permute-start.51 = (bf16[4,16,1024]{2,1,0:T(8,128)(2,1)S(1)}, bf16[4,16,1024]{2,1,0:T(8,128)(2,1)}, u32[]{:S(2)}, u32[]{:S(2)}) collective-permute-start(bf16[4,16,1024]{2,1,0:T(8,128)(2,1)S(1)} %get-tuple-element.277), channel_id=1, source_target_pairs={{0,24},{8,16},{16,8},{24,0},{1,25},{9,17},{17,9},{25,1},{2,26},{10... | collective-permute-start | bytes 393224 | tf_op jit(solution)/shard_map/cond/branch_8_fun/ppermute | solution.py:158
  42.1 4.6 %collective-permute-done.48 = bf16[576,256]{1,0:T(8,128)(2,1)} collective-permute-done((bf16[576,256]{1,0:T(8,128)(2,1)S(1)}, bf16[576,256]{1,0:T(8,128)(2,1)}, u32[]{:S(2)}, u32[]{:S(2)}) %collective-permute-start.48) | collective-permute-done | bytes 294944 | tf_op jit(solution)/shard_map/cond/branch_8_fun/ppermute | solution.py:251
  46.7 0.0 collective-permute-done.51
  46.7 0.1 collective-permute-start.53
  46.8 0.5 collective-permute-start.52
  47.3 9.9 %collective-permute-done.52 = bf16[576,256]{1,0:T(8,128)(2,1)} collective-permute-done((bf16[576,256]{1,0:T(8,128)(2,1)S(1)}, bf16[576,256]{1,0:T(8,128)(2,1)}, u32[]{:S(2)}, u32[]{:S(2)}) %collective-permute-start.52) | collective-permute-done | bytes 294944 | tf_op jit(solution)/shard_map/cond/branch_8_fun/ppermute | solution.py:254
  57.2 1.2 %fusion.7 = (bf16[4,16,1024]{2,1,0:T(8,128)(2,1)S(1)}, f32[4,16,1024]{2,1,0:T(8,128)S(1)}) fusion(bf16[4,16,1024]{2,1,0:T(8,128)(2,1)} %get-tuple-element.395, bf16[4,16,1024]{2,1,0:T(8,128)(2,1)} %get-tuple-element.394, f32[4,16,1024]{2,1,0:T(8,128)S(1)} %get-tuple-element.385, bf16[4,16,1024]{2,1,0:T(8,128)(2,1)} %get-tuple-element.393), kind=kLoop, calls=%fused_computation.45 | loop fusion | flops 458752 | bytes 1048576 | tf_op jit(solution)/shard_map/convert_element_type | solution.py:298
  58.4 0.1 collective-permute-start.95
  58.5 0.1 collective-permute-start.96
  58.5 4.3 %collective-permute-start.97 = (bf16[16,1024]{1,0:T(8,128)(2,1)S(1)}, bf16[16,1024]{1,0:T(8,128)(2,1)S(1)}, u32[]{:S(2)}, u32[]{:S(2)}) collective-permute-start(bf16[16,1024]{1,0:T(8,128)(2,1)S(1)} %get-tuple-element.404), channel_id=1, source_target_pairs={{0,6},{1,7},{2,4},{3,5},{4,2},{5,3},{6,0},{7,1},{8,14},{9,15},{10,... | collective-permute-start | bytes 98312 | tf_op jit(solution)/shard_map/ppermute | solution.py:158
  62.8 0.1 copy.10.relocate_ref
  62.9 3.0 %weight_grads.1 = (bf16[384,1024]{1,0:T(8,128)(2,1)}, bf16[192,1024]{1,0:T(8,128)(2,1)}) custom-call(s32[8,1]{1,0:T(8,128)S(1)} %copy.10.relocate_ref, bf16[576,256]{1,0:T(8,128)(2,1)} %get-tuple-element.396.same_ref, bf16[576,256]{1,0:T(8,128)(2,1)} %get-tuple-element.397.cross_ref, bf16[256,2176]{1,0:T(8,128)(2,1)S(1)} %copy-done.3, ...), custom_call_target="tpu_custom_call" | custom-call | tf_op jit(solution)/shard_map/weight_grads/pallas_call | solution.py:302
  66.0 0.6 fusion.3
  (20 shorter events, 0.1 us)
Async XLA Ops:
  3.5 8.8 %collective-permute-start.84 = (bf16[16,2176]{1,0:T(8,128)(2,1)S(1)}, bf16[16,2176]{1,0:T(8,128)(2,1)S(1)}, u32[]{:S(2)}, u32[]{:S(2)}) collective-permute-start(bf16[16,2176]{1,0:T(8,128)(2,1)S(1)} %pad_maximum_fusion.refs_0_), channel_id=1, source_target_pairs={{0,2},{1,3},{2,0},{3,1},{4,6},{5,7},{6,4},{7,5},{8,10},{9,11},{10,... | collective-permute-start | bytes 208904 | tf_op jit(solution)/shard_map/ppermute | solution.py:158
  6.5 7.5 %collective-permute-start.85 = (bf16[16,2176]{1,0:T(8,128)(2,1)S(1)}, bf16[16,2176]{1,0:T(8,128)(2,1)S(1)}, u32[]{:S(2)}, u32[]{:S(2)}) collective-permute-start(bf16[16,2176]{1,0:T(8,128)(2,1)S(1)} %pad_maximum_fusion.refs_0_), channel_id=1, source_target_pairs={{0,4},{1,5},{2,6},{3,7},{4,0},{5,1},{6,2},{7,3},{8,12},{9,13},{10,... | collective-permute-start | bytes 208904 | tf_op jit(solution)/shard_map/ppermute | solution.py:158
  9.1 6.2 %collective-permute-start.86 = (bf16[16,2176]{1,0:T(8,128)(2,1)S(1)}, bf16[16,2176]{1,0:T(8,128)(2,1)S(1)}, u32[]{:S(2)}, u32[]{:S(2)}) collective-permute-start(bf16[16,2176]{1,0:T(8,128)(2,1)S(1)} %pad_maximum_fusion.refs_0_), channel_id=1, source_target_pairs={{0,6},{1,7},{2,4},{3,5},{4,2},{5,3},{6,0},{7,1},{8,14},{9,15},{10,... | collective-permute-start | bytes 208904 | tf_op jit(solution)/shard_map/ppermute | solution.py:158
  9.1 6.2 %collective-permute-start.87 = (bf16[16,2176]{1,0:T(8,128)(2,1)S(1)}, bf16[16,2176]{1,0:T(8,128)(2,1)S(1)}, u32[]{:S(2)}, u32[]{:S(2)}) collective-permute-start(bf16[16,2176]{1,0:T(8,128)(2,1)S(1)} %pad_maximum_fusion.refs_0_), channel_id=1, source_target_pairs={{0,8},{8,0},{16,24},{24,16},{1,9},{9,1},{17,25},{25,17},{2,10},{10... | collective-permute-start | bytes 208904 | tf_op jit(solution)/shard_map/ppermute | solution.py:158
  10.9 5.0 %collective-permute-start.88 = (bf16[16,2176]{1,0:T(8,128)(2,1)S(1)}, bf16[16,2176]{1,0:T(8,128)(2,1)S(1)}, u32[]{:S(2)}, u32[]{:S(2)}) collective-permute-start(bf16[16,2176]{1,0:T(8,128)(2,1)S(1)} %pad_maximum_fusion.refs_0_), channel_id=1, source_target_pairs={{0,16},{8,24},{16,0},{24,8},{1,17},{9,25},{17,1},{25,9},{2,18},{10... | collective-permute-start | bytes 208904 | tf_op jit(solution)/shard_map/ppermute | solution.py:158
  12.4 5.2 %collective-permute-start.89 = (bf16[16,2176]{1,0:T(8,128)(2,1)S(1)}, bf16[16,2176]{1,0:T(8,128)(2,1)S(1)}, u32[]{:S(2)}, u32[]{:S(2)}) collective-permute-start(bf16[16,2176]{1,0:T(8,128)(2,1)S(1)} %pad_maximum_fusion.refs_0_), channel_id=1, source_target_pairs={{0,24},{8,16},{16,8},{24,0},{1,25},{9,17},{17,9},{25,1},{2,26},{10... | collective-permute-start | bytes 208904 | tf_op jit(solution)/shard_map/ppermute | solution.py:158
  17.6 12.5 %collective-permute-start.93 = (bf16[384,1024]{1,0:T(8,128)(2,1)}, bf16[384,1024]{1,0:T(8,128)(2,1)S(1)}, u32[]{:S(2)}, u32[]{:S(2)}) collective-permute-start(bf16[384,1024]{1,0:T(8,128)(2,1)} %bitcast.56), channel_id=1, source_target_pairs={{0,1},{1,0},{2,3},{3,2},{4,5},{5,4},{6,7},{7,6},{8,9},{9,8},{10,11... | collective-permute-start | bytes 2359304 | tf_op jit(solution)/shard_map/ppermute | solution.py:158
  17.6 12.5 %collective-permute-start.94 = (bf16[192,1024]{1,0:T(8,128)(2,1)}, bf16[192,1024]{1,0:T(8,128)(2,1)S(1)}, u32[]{:S(2)}, u32[]{:S(2)}) collective-permute-start(bf16[192,1024]{1,0:T(8,128)(2,1)} %bitcast.58), channel_id=1, source_target_pairs={{0,1},{1,0},{2,3},{3,2},{4,5},{5,4},{6,7},{7,6},{8,9},{9,8},{10,11... | collective-permute-start | bytes 1179656 | tf_op jit(solution)/shard_map/ppermute | solution.py:158
  18.1 8.1 %collective-permute-start.90 = (bf16[48,2176]{1,0:T(8,128)(2,1)S(1)}, bf16[48,2176]{1,0:T(8,128)(2,1)S(1)}, u32[]{:S(2)}, u32[]{:S(2)}) collective-permute-start(bf16[48,2176]{1,0:T(8,128)(2,1)S(1)} %constant_dynamic-update-slice_fusion), channel_id=1, source_target_pairs={{0,8},{8,0},{16,24},{24,16},{1,9},{9,1},{17,25},{25,17},{2,10},{10... | collective-permute-start | bytes 626696 | tf_op jit(solution)/shard_map/ppermute | solution.py:158
  18.7 11.3 %collective-permute-start.91 = (bf16[48,2176]{1,0:T(8,128)(2,1)S(1)}, bf16[48,2176]{1,0:T(8,128)(2,1)S(1)}, u32[]{:S(2)}, u32[]{:S(2)}) collective-permute-start(bf16[48,2176]{1,0:T(8,128)(2,1)S(1)} %constant_dynamic-update-slice_fusion), channel_id=1, source_target_pairs={{0,16},{8,24},{16,0},{24,8},{1,17},{9,25},{17,1},{25,9},{2,18},{10... | collective-permute-start | bytes 626696 | tf_op jit(solution)/shard_map/ppermute | solution.py:158
  19.1 11.0 %collective-permute-start.92 = (bf16[48,2176]{1,0:T(8,128)(2,1)S(1)}, bf16[48,2176]{1,0:T(8,128)(2,1)S(1)}, u32[]{:S(2)}, u32[]{:S(2)}) collective-permute-start(bf16[48,2176]{1,0:T(8,128)(2,1)S(1)} %constant_dynamic-update-slice_fusion), channel_id=1, source_target_pairs={{0,24},{8,16},{16,8},{24,0},{1,25},{9,17},{17,9},{25,1},{2,26},{10... | collective-permute-start | bytes 626696 | tf_op jit(solution)/shard_map/ppermute | solution.py:158
  30.1 1.1 %copy-start = (bf16[1,1,384,1024]{3,2,1,0:T(8,128)(2,1)S(1)}, bf16[1,1,384,1024]{3,2,1,0:T(8,128)(2,1)}, u32[]{:S(2)}) copy-start(bf16[1,1,384,1024]{3,2,1,0:T(8,128)(2,1)} %param.26) | copy-start | bytes 2359300
  31.2 1.0 %copy-start.1 = (bf16[1,1,192,1024]{3,2,1,0:T(8,128)(2,1)S(1)}, bf16[1,1,192,1024]{3,2,1,0:T(8,128)(2,1)}, u32[]{:S(2)}) copy-start(bf16[1,1,192,1024]{3,2,1,0:T(8,128)(2,1)} %param.27) | copy-start | bytes 1179652
  33.9 1.0 %copy-start.2 = (bf16[256,2176]{1,0:T(8,128)(2,1)}, bf16[256,2176]{1,0:T(8,128)(2,1)S(1)}, u32[]{:S(2)}) copy-start(bf16[256,2176]{1,0:T(8,128)(2,1)S(1)} %get-tuple-element.392.plane_ref) | copy-start | bytes 3342340
  33.9 28.9 %copy-start.4 = (s32[8,1]{0,1:T(1,128)S(1)}, s32[8,1]{0,1:T(1,128)}, u32[]{:S(2)}) copy-start(s32[8,1]{0,1:T(1,128)} %param.25) | copy-start | bytes 100
  35.0 11.7 %collective-permute-start.48 = (bf16[576,256]{1,0:T(8,128)(2,1)S(1)}, bf16[576,256]{1,0:T(8,128)(2,1)}, u32[]{:S(2)}, u32[]{:S(2)}) collective-permute-start(bf16[576,256]{1,0:T(8,128)(2,1)S(1)} %get-tuple-element.272), channel_id=1, source_target_pairs={{0,4},{1,1},{2,2},{3,7},{4,0},{5,5},{6,6},{7,3},{8,12},{9,9},{10,1... | collective-permute-start | bytes 884744 | tf_op jit(solution)/shard_map/cond/branch_8_fun/ppermute | solution.py:251
  38.6 8.1 %collective-permute-start.49 = (bf16[4,16,1024]{2,1,0:T(8,128)(2,1)S(1)}, bf16[4,16,1024]{2,1,0:T(8,128)(2,1)}, u32[]{:S(2)}, u32[]{:S(2)}) collective-permute-start(bf16[4,16,1024]{2,1,0:T(8,128)(2,1)S(1)} %get-tuple-element.275), channel_id=1, source_target_pairs={{0,8},{8,0},{16,24},{24,16},{1,9},{9,1},{17,25},{25,17},{2,10},{10... | collective-permute-start | bytes 393224 | tf_op jit(solution)/shard_map/cond/branch_8_fun/ppermute | solution.py:158
  40.1 6.6 %collective-permute-start.50 = (bf16[4,16,1024]{2,1,0:T(8,128)(2,1)S(1)}, bf16[4,16,1024]{2,1,0:T(8,128)(2,1)}, u32[]{:S(2)}, u32[]{:S(2)}) collective-permute-start(bf16[4,16,1024]{2,1,0:T(8,128)(2,1)S(1)} %get-tuple-element.276), channel_id=1, source_target_pairs={{0,16},{8,24},{16,0},{24,8},{1,17},{9,25},{17,1},{25,9},{2,18},{10... | collective-permute-start | bytes 393224 | tf_op jit(solution)/shard_map/cond/branch_8_fun/ppermute | solution.py:158
  40.6 6.1 %collective-permute-start.51 = (bf16[4,16,1024]{2,1,0:T(8,128)(2,1)S(1)}, bf16[4,16,1024]{2,1,0:T(8,128)(2,1)}, u32[]{:S(2)}, u32[]{:S(2)}) collective-permute-start(bf16[4,16,1024]{2,1,0:T(8,128)(2,1)S(1)} %get-tuple-element.277), channel_id=1, source_target_pairs={{0,24},{8,16},{16,8},{24,0},{1,25},{9,17},{17,9},{25,1},{2,26},{10... | collective-permute-start | bytes 393224 | tf_op jit(solution)/shard_map/cond/branch_8_fun/ppermute | solution.py:158
  46.7 10.5 %collective-permute-start.53 = (bf16[256,2176]{1,0:T(8,128)(2,1)S(1)}, bf16[256,2176]{1,0:T(8,128)(2,1)}, u32[]{:S(2)}, u32[]{:S(2)}) collective-permute-start(bf16[256,2176]{1,0:T(8,128)(2,1)S(1)} %get-tuple-element.281), channel_id=1, source_target_pairs={{0,1},{1,0},{2,3},{3,2},{4,5},{5,4},{6,7},{7,6},{8,9},{9,8},{10,11... | collective-permute-start | bytes 3342344 | tf_op jit(solution)/shard_map/cond/branch_8_fun/ppermute | solution.py:158
  46.8 10.4 %collective-permute-start.52 = (bf16[576,256]{1,0:T(8,128)(2,1)S(1)}, bf16[576,256]{1,0:T(8,128)(2,1)}, u32[]{:S(2)}, u32[]{:S(2)}) collective-permute-start(bf16[576,256]{1,0:T(8,128)(2,1)S(1)} %get-tuple-element.280), channel_id=1, source_target_pairs={{0,1},{1,4},{2,7},{3,2},{4,5},{5,0},{6,3},{7,6},{8,9},{9,12},{10,1... | collective-permute-start | bytes 884744 | tf_op jit(solution)/shard_map/cond/branch_8_fun/ppermute | solution.py:254
  57.2 5.8 %copy-start.3 = (bf16[256,2176]{1,0:T(8,128)(2,1)S(1)}, bf16[256,2176]{1,0:T(8,128)(2,1)}, u32[]{:S(2)}) copy-start(bf16[256,2176]{1,0:T(8,128)(2,1)} %copy-done.2) | copy-start | bytes 3342340
  58.4 7.6 %collective-permute-start.95 = (bf16[16,1024]{1,0:T(8,128)(2,1)S(1)}, bf16[16,1024]{1,0:T(8,128)(2,1)S(1)}, u32[]{:S(2)}, u32[]{:S(2)}) collective-permute-start(bf16[16,1024]{1,0:T(8,128)(2,1)S(1)} %get-tuple-element.403), channel_id=1, source_target_pairs={{0,2},{1,3},{2,0},{3,1},{4,6},{5,7},{6,4},{7,5},{8,10},{9,11},{10,... | collective-permute-start | bytes 98312 | tf_op jit(solution)/shard_map/ppermute | solution.py:158
  58.5 7.5 %collective-permute-start.96 = (bf16[16,1024]{1,0:T(8,128)(2,1)S(1)}, bf16[16,1024]{1,0:T(8,128)(2,1)S(1)}, u32[]{:S(2)}, u32[]{:S(2)}) collective-permute-start(bf16[16,1024]{1,0:T(8,128)(2,1)S(1)} %get-tuple-element.405), channel_id=1, source_target_pairs={{0,4},{1,5},{2,6},{3,7},{4,0},{5,1},{6,2},{7,3},{8,12},{9,13},{10,... | collective-permute-start | bytes 98312 | tf_op jit(solution)/shard_map/ppermute | solution.py:158
  58.5 7.4 %collective-permute-start.97 = (bf16[16,1024]{1,0:T(8,128)(2,1)S(1)}, bf16[16,1024]{1,0:T(8,128)(2,1)S(1)}, u32[]{:S(2)}, u32[]{:S(2)}) collective-permute-start(bf16[16,1024]{1,0:T(8,128)(2,1)S(1)} %get-tuple-element.404), channel_id=1, source_target_pairs={{0,6},{1,7},{2,4},{3,5},{4,2},{5,3},{6,0},{7,1},{8,14},{9,15},{10,... | collective-permute-start | bytes 98312 | tf_op jit(solution)/shard_map/ppermute | solution.py:158

commit v3 on v2

--- a/solution.py
+++ b/solution.py
@@ -175,10 +175,41 @@
     return jnp.concatenate([tokens, upstream, table.astype(jnp.bfloat16)], axis=1)
 
 
-def forward_kernel(n_cols, n_rows, n_z, *refs):
+def gate_rows_of(plane, columns, n_cols, wanted):
+    lane = lax.broadcasted_iota(jnp.int32, (8, 128), 1)
+    row = lax.broadcasted_iota(jnp.int32, (8, 128), 0)
+    chosen = jnp.zeros((8, 128), jnp.bool_)
+    for index, expert in enumerate(wanted):
+        chosen |= (row == index) & (lane % n_cols == expert) & (lane < 3 * n_cols)
+    return lax.dot_general(
+        jnp.where(chosen, 1.0, 0.0).astype(jnp.bfloat16), plane[:, columns:], contract_last, preferred_element_type=jnp.float32
+    )
+
+
+def activations(gate_weights, up_weights, down_weights, rows_x, rows_u, gate):
+    gate_pre = lax.dot_general(gate_weights, rows_x, contract_last, preferred_element_type=jnp.float32)
+    up_pre = lax.dot_general(up_weights, rows_x, contract_last, preferred_element_type=jnp.float32)
+    hidden_grad = gate * lax.dot_general(down_weights, rows_u, contract_last, preferred_element_type=jnp.float32)
+    activated, slope_of = silu_parts(gate_pre)
+    return (
+        (hidden_grad * up_pre * slope_of).astype(jnp.bfloat16),
+        (hidden_grad * activated).astype(jnp.bfloat16),
+        (activated * up_pre * gate).astype(jnp.bfloat16),
+    )
+
+
+def forward_kernel(n_cols, n_rows, n_z, early, *refs):
     near = refs[: n_rows + n_z - 1]
     far = refs[n_rows + n_z - 1 : 2 * n_rows + n_z - 2]
-    wgu_own, wdn_own, wgu_sib, wdn_sib, plane_ref, own_ref, sib_ref, kept_ref, *sent_refs = refs[2 * n_rows + n_z - 2 :]
+    wgu_hbm, wdn_hbm, wgu_sib, wdn_sib, plane_out, own_ref, sib_ref, kept_ref, *rest = refs[2 * n_rows + n_z - 2 :]
+    sent_refs = rest[: n_rows - 1]
+    plane_ref, wgu_own, wdn_own, acts_ref, sems = rest[n_rows - 1 :]
+    loads = [
+        pltpu.make_async_copy(wgu_hbm, wgu_own, sems.at[0]),
+        pltpu.make_async_copy(wdn_hbm, wdn_own, sems.at[1]),
+    ]
+    for load in loads:
+        load.start()
     tok_dev = near[0].shape[0]
     for z in range(n_z):
         for d in range(n_rows):
@@ -190,28 +221,25 @@
             else:
                 block = far[d - 1][(z - 1) * tok_dev : z * tok_dev]
             plane_ref[start : start + tok_dev] = block
-    units, width = wdn_own.shape
+    keep = pltpu.make_async_copy(plane_ref, plane_out, sems.at[2])
+    keep.start()
+    units, width = wdn_sib.shape
     col_here = lax.axis_index("expert")
-    lane = lax.broadcasted_iota(jnp.int32, (8, 128), 1)
-    row = lax.broadcasted_iota(jnp.int32, (8, 128), 0)
-    wanted = jnp.where(row == 0, col_here, col_here ^ 1)
-    chosen = (row < 2) & (lane % n_cols == wanted) & (lane < 3 * n_cols)
-    gate_rows = lax.dot_general(
-        jnp.where(chosen, 1.0, 0.0).astype(jnp.bfloat16), plane_ref[:, 2 * width :], contract_last, preferred_element_type=jnp.float32
-    )
+    gate_rows = gate_rows_of(plane_ref, 2 * width, n_cols, (col_here ^ 1, col_here))
+    rows_x = plane_ref[:, :width]
+    rows_u = plane_ref[:, width : 2 * width]
     total = None
-    for index, (wgu, wdn, acts_ref) in enumerate(((wgu_own, wdn_own, own_ref), (wgu_sib, wdn_sib, sib_ref))):
-        gate = gate_rows[index : index + 1, :]
-        pre = lax.dot_general(wgu[...], plane_ref[:, :width], contract_last, preferred_element_type=jnp.float32)
-        hidden_grad = gate * lax.dot_general(
-            wdn[...], plane_ref[:, width : 2 * width], contract_last, preferred_element_type=jnp.float32
-        )
-        activated, slope_of = silu_parts(pre[:units])
-        up_pre = pre[units:]
-        acts_ref[:units] = (hidden_grad * up_pre * slope_of).astype(jnp.bfloat16)
-        acts_ref[units : 2 * units] = (hidden_grad * activated).astype(jnp.bfloat16)
-        acts_ref[2 * units :] = (activated * up_pre * gate).astype(jnp.bfloat16)
-        part = lax.dot_general(acts_ref[: 2 * units], wgu[...], contract_first, preferred_element_type=jnp.float32)
+    for index, (wgu, wdn, late_ref) in enumerate(((wgu_sib, wdn_sib, sib_ref), (wgu_own, wdn_own, own_ref))):
+        if index == 1:
+            for load in loads:
+                load.wait()
+        parts = activations(wgu[:units], wgu[units:], wdn[...], rows_x, rows_u, gate_rows[index : index + 1, :])
+        late = units - early
+        for i, part in enumerate(parts):
+            late_ref[i * late : (i + 1) * late] = part[early:]
+        acts_ref[:units] = parts[0]
+        acts_ref[units:] = parts[1]
+        part = lax.dot_general(acts_ref[...], wgu[...], contract_first, preferred_element_type=jnp.float32)
         total = part if total is None else total + part
     for z in range(n_z):
         for d in range(n_rows):
@@ -221,24 +249,38 @@
                 kept_ref[z] = block
             else:
                 sent_refs[d - 1][z] = block.astype(jnp.bfloat16)
+    keep.wait()
+
+
+def weight_grad_kernel(
+    n_cols, relocate_ref, same_ref, cross_ref, early_own, early_got, plane_ref, other_ref, gu_ref, dn_ref, weights, gate_acts, up_acts, down_acts
+):
+    units, width = dn_ref.shape
+    early = early_own.shape[0] // 3
+    late = units - early
+    col_here = lax.axis_index("expert")
+    moved = relocate_ref[col_here, 0] == 1
+    weights[...] = jnp.where(moved, early_got[...], early_own[...])
+    source = jnp.where(moved, col_here ^ (n_cols // 2), col_here)
+    for side, (late_ref, rows) in enumerate(((same_ref, plane_ref), (cross_ref, other_ref))):
+        gate = gate_rows_of(rows, 2 * width, n_cols, (source,))[:1, :]
+        parts = activations(
+            weights[:early], weights[early : 2 * early], weights[2 * early :], rows[:, :width], rows[:, width : 2 * width], gate
+        )
+        late_acts = jnp.where(moved, halves_swapped(late_ref[...]), late_ref[...])
+        for i, acts in enumerate((gate_acts, up_acts, down_acts)):
+            acts[side, :early] = parts[i]
+            acts[side, early:] = late_acts[i * late : (i + 1) * late]
+    for out, acts, start in ((gu_ref.at[:units], gate_acts, 0), (gu_ref.at[units:], up_acts, 0), (dn_ref, down_acts, width)):
+        out[...] = (
+            jnp.dot(acts[0], plane_ref[:, start : start + width], preferred_element_type=jnp.float32)
+            + jnp.dot(acts[1], other_ref[:, start : start + width], preferred_element_type=jnp.float32)
+        ).astype(jnp.bfloat16)
 
 
 def halves_swapped(acts):
     half = acts.shape[1] // 2
     return jnp.concatenate([acts[:, half:], acts[:, :half]], axis=1)
-
-
-def weight_grad_kernel(relocate_ref, same_ref, cross_ref, plane_ref, other_ref, gu_ref, dn_ref):
-    units, width = dn_ref.shape
-    moved = relocate_ref[lax.axis_index("expert"), 0] == 1
-    same = jnp.where(moved, halves_swapped(same_ref[...]), same_ref[...])
-    cross = jnp.where(moved, halves_swapped(cross_ref[...]), cross_ref[...])
-    for out, low, start in ((gu_ref, 0, 0), (dn_ref, 2 * units, width)):
-        high = low + out.shape[0]
-        out[...] = (
-            jnp.dot(same[low:high], plane_ref[:, start : start + width], preferred_element_type=jnp.float32)
-            + jnp.dot(cross[low:high], other_ref[:, start : start + width], preferred_element_type=jnp.float32)
-        ).astype(jnp.bfloat16)
 
 
 def exchanges(pattern, acts_own, acts_sib, plane, sent_rows):
@@ -268,30 +310,44 @@
     limit = pltpu.CompilerParams(vmem_limit_bytes=16 * 2**20)
     bf16 = jnp.bfloat16
 
+    early = units // 3 // 16 * 16
+    wgu_own, wdn_own = w_gate_up[0, 0], w_down[0, 0]
+    wgu_sib = crossed(wgu_own, "expert", 1)
+    wdn_sib = crossed(wdn_own, "expert", 1)
     own = packed(tokens, upstream, expert_ids, gates, n_cols)
+    own, wgu_sib, wdn_sib, w_gate_up, w_down = lax.optimization_barrier((own, wgu_sib, wdn_sib, w_gate_up, w_down))
+    early_own = jnp.concatenate(
+        [w_gate_up[0, 0, :early], w_gate_up[0, 0, units : units + early], w_down[0, 0, :early]], axis=0
+    )
 
     along_dp = [crossed(own, "dp", d) for d in range(1, n_rows)]
     along_z = [crossed(own, "expert", 2 * dz) for dz in range(1, n_z)]
     bits = jnp.sum(relocate[:half, 0] << jnp.arange(half, dtype=jnp.int32))
-    along_z, along_dp, w_gate_up, w_down, bits = lax.optimization_barrier((along_z, along_dp, w_gate_up, w_down, bits))
+    along_z, along_dp, early_own, bits = lax.optimization_barrier((along_z, along_dp, early_own, bits))
     far = jnp.concatenate(along_z, axis=0)
     far_dp = [crossed(far, "dp", d) for d in range(1, n_rows)]
-    wgu_own, wdn_own = w_gate_up[0, 0], w_down[0, 0]
-    wgu_sib = crossed(wgu_own, "expert", 1)
-    wdn_sib = crossed(wdn_own, "expert", 1)
-    acts = jax.ShapeDtypeStruct((3 * units, plane_rows), bf16)
+    early_got = crossed(early_own, "expert", half)
+    acts = jax.ShapeDtypeStruct((3 * (units - early), plane_rows), bf16)
     plane, acts_own, acts_sib, kept, *sent = pl.pallas_call(
-        functools.partial(forward_kernel, n_cols, n_rows, n_z),
+        functools.partial(forward_kernel, n_cols, n_rows, n_z, early),
         out_shape=[jax.ShapeDtypeStruct((plane_rows, own.shape[1]), bf16), acts, acts, jax.ShapeDtypeStruct((n_z, tok_dev, width), jnp.float32)]
         + [jax.ShapeDtypeStruct((n_z, tok_dev, width), bf16)] * (n_rows - 1),
-        in_specs=whole(2 * n_rows + n_z + 2),
-        out_specs=whole(3 + n_rows),
+        in_specs=whole(2 * n_rows + n_z - 2) + [pl.BlockSpec(memory_space=pl.ANY)] * 2 + whole(2),
+        out_specs=[pl.BlockSpec(memory_space=pl.ANY)] + whole(2 + n_rows),
+        scratch_shapes=[
+            pltpu.VMEM((plane_rows, own.shape[1]), bf16),
+            pltpu.VMEM(wgu_own.shape, bf16),
+            pltpu.VMEM(wdn_own.shape, bf16),
+            pltpu.VMEM((2 * units, plane_rows), bf16),
+            pltpu.SemaphoreType.DMA((3,)),
+        ],
         compiler_params=limit,
         name="forward",
     )(own, *along_dp, *along_z, *far_dp, wgu_own, wdn_own, wgu_sib, wdn_sib)
 
     branches = [functools.partial(exchanges, pattern) for pattern in range(1, (1 << half) - 1)]
     got_same, got_cross, plane_sib, got = lax.switch(bits - 1, branches, acts_own, acts_sib, plane, sent)
+    got, early_got = lax.optimization_barrier((got, early_got))
     total = kept
     for block in got:
         total = total + block.astype(jnp.float32)
@@ -300,13 +356,14 @@
     for dz in range(1, n_z):
         grad_tokens = grad_tokens + crossed(sent_total[dz], "expert", 2 * dz).astype(jnp.float32)
     grad_gu, grad_dn = pl.pallas_call(
-        weight_grad_kernel,
+        functools.partial(weight_grad_kernel, n_cols),
         out_shape=[jax.ShapeDtypeStruct((2 * units, width), bf16), jax.ShapeDtypeStruct((units, width), bf16)],
-        in_specs=[pl.BlockSpec(memory_space=pltpu.SMEM)] + whole(4),
+        in_specs=[pl.BlockSpec(memory_space=pltpu.SMEM)] + whole(6),
         out_specs=whole(2),
+        scratch_shapes=[pltpu.VMEM(early_own.shape, bf16)] + [pltpu.VMEM((2, units, plane_rows), bf16)] * 3,
         compiler_params=limit,
         name="weight_grads",
-    )(relocate, got_same, got_cross, plane, plane_sib)
+    )(relocate, got_same, got_cross, early_own, early_got, plane, plane_sib)
     return grad_tokens.astype(bf16), grad_gu.reshape(w_gate_up.shape), grad_dn.reshape(w_down.shape)
 
 

time: 67.5 us -> 71 us (1.052); the launches traced: 66.6 us -> 70.8 us
  waiting for transfers between devices: 25.9 us -> 19.8 us
  local copies, waits for them, and re-layouts: 5.22 us -> 10.6 us
  Pallas kernels: 4.75 us -> 8.2 us
  starting transfers between devices: 25.3 us -> 26.7 us
    ppermute x1, waiting for transfers between devices: 9.87 us -> 5.59 us  [exchanges(): lax.ppermute(acts_sib, 'expert', [(col, place(col ^ 1)) for col in range(...]
    pallas_call x2, Pallas kernels: 4.75 us -> 8.2 us  [the longest x1 4.26 us: dense_device(): pl.pallas_call(functools.partial(weight_grad_kernel, n_cols), out_shape=[...]
    unnamed x13 -> x23, local copies, waits for them, and re-layouts: 3.23 us -> 6.08 us
    ppermute x1, waiting for transfers between devices: 4.59 us -> 1.8 us  [exchanges(): lax.ppermute(acts_own, 'expert', [(col, place(col)) for col in range(n_co...]
    squeeze x0 -> x2, local copies, waits for them, and re-layouts: none -> 1.9 us  [the longest x1 0.98 us: dense_device(): w_gate_up[0, 0, :early]]
    ppermute x18 -> x19, starting transfers between devices: 21.2 us -> 23 us  [crossed(): lax.ppermute(block, axis, [(i, i ^ apart) for i in range(lax.axis_size(ax...]
    ppermute x18 -> x19, waiting for transfers between devices: 11.4 us -> 12.4 us  [crossed(): lax.ppermute(block, axis, [(i, i ^ apart) for i in range(lax.axis_size(ax...]
  transfers between devices with their start and end apart: 20 -> 21, of which waited for: 8 -> 8; matrix products, arithmetic and copies ran while one was open for 2% -> 11% of each run, Pallas kernels for 5% -> 12%
where the time goes in v3:
time: 71 us; the launch traced here: 70.8 us
  starting transfers between devices  26.7 us (38%)
  waiting for transfers between devices  19.8 us (28%)
  local copies, waits for them, and re-layouts  10.6 us (15%)
  Pallas kernels  8.2 us (12%)
  other arithmetic  4.12 us (6%)
  between operations  1.43 us (2%)
    ppermute x19, starting transfers between devices, crossed(): lax.ppermute(block, axis, [(i, i ^ apart) for i in range(lax.axis_size(ax...  23 us
    ppermute x19, waiting for transfers between devices, crossed(): lax.ppermute(block, axis, [(i, i ^ apart) for i in range(lax.axis_size(ax...  12.4 us
    unnamed x23, local copies, waits for them, and re-layouts  6.08 us
    ppermute x1, waiting for transfers between devices, exchanges(): lax.ppermute(acts_sib, 'expert', [(col, place(col ^ 1)) for col in range(...  5.59 us
    pallas_call x1, Pallas kernels, dense_device(): pl.pallas_call(functools.partial(weight_grad_kernel, n_cols), out_shape=[...  4.26 us
    pallas_call x1, Pallas kernels, dense_device(): pl.pallas_call(functools.partial(forward_kernel, n_cols, n_rows, n_z, ear...  3.93 us
    ppermute x1, starting transfers between devices, exchanges(): lax.ppermute(acts_own, 'expert', [(col, place(col)) for col in range(n_co...  3.2 us
    ppermute x1, waiting for transfers between devices, exchanges(): lax.ppermute(acts_own, 'expert', [(col, place(col)) for col in range(n_co...  1.8 us
  transfers between devices with their start and end apart: 21, of which 8 were waited for; matrix products, arithmetic and copies ran while one was open for 11% of the time, Pallas kernels for 12%

profile of v3, /device:TPU:0, one launch (start us, length us, event | category | flops | bytes accessed | tf_op | source)
XLA Modules:
  0.0 70.8 jit_solution(1279504985038069000)
XLA Ops:
  0.7 0.5 collective-permute-start.84
  1.2 0.1 collective-permute-start.85
  1.3 1.0 %slice_bitcast_fusion.22 = (s32[16]{0:T(128)S(1)}, s32[16]{0:T(128)S(1)}, s32[16]{0:T(128)S(1)}, s32[16]{0:T(128)S(1)}, s32[16]{0:T(128)S(1)}, /*index=5*/s32[16]{0:T(128)S(1)}, s32[16]{0:T(128)S(1)}, s32[16]{0:T(128)S(1)}) fusion(s32[16,8]{0,1:T(8,128)} %param.23), kind=kLoop, calls=%fused_computation.45 | loop fusion | bytes 1024 | tf_op jit(solution)/shard_map/eq | solution.py:170
  2.2 1.0 %slice_bitcast_fusion.21 = (f32[16]{0:T(128)S(1)}, f32[16]{0:T(128)S(1)}, f32[16]{0:T(128)S(1)}, f32[16]{0:T(128)S(1)}, f32[16]{0:T(128)S(1)}, /*index=5*/f32[16]{0:T(128)S(1)}, f32[16]{0:T(128)S(1)}, f32[16]{0:T(128)S(1)}) fusion(f32[16,8]{0,1:T(8,128)} %param.24), kind=kLoop, calls=%fused_computation.44 | loop fusion | bytes 1024 | tf_op jit(solution)/shard_map/jit(_where)/broadcast_in_dim | solution.py:170
  3.2 0.1 fusion.4
  3.4 1.3 %fusion.6 = s32[]{:T(128)} fusion(s32[8,1]{0,1:T(1,128)} %param.25), kind=kLoop, calls=%fused_computation.29 | loop fusion | flops 7 | bytes 20 | tf_op jit(solution)/shard_map/reduce_sum | solution.py:325
  4.6 0.8 %pad_maximum_fusion.1.refs_0_ = bf16[16,2176]{1,0:T(8,128)(2,1)S(1)} fusion(bf16[16,128]{1,0:T(8,128)(2,1)S(1)} %fusion.4, bf16[16,1024]{1,0:T(8,128)(2,1)} %param.22, bf16[16,1024]{1,0:T(8,128)(2,1)} %param.21), kind=kLoop, calls=%fused_computation.5 | loop fusion | flops 208896 | bytes 139264 | tf_op jit(solution)/shard_map/concatenate | solution.py:175
  5.4 3.1 %collective-permute-start.86 = (bf16[16,2176]{1,0:T(8,128)(2,1)S(1)}, bf16[16,2176]{1,0:T(8,128)(2,1)S(1)}, u32[]{:S(2)}, u32[]{:S(2)}) collective-permute-start(bf16[16,2176]{1,0:T(8,128)(2,1)S(1)} %pad_maximum_fusion.1.refs_0_), channel_id=1, source_target_pairs={{0,2},{1,3},{2,0},{3,1},{4,6},{5,7},{6,4},{7,5},{8,10},{9,11},{10,... | collective-permute-start | bytes 208904 | tf_op jit(solution)/shard_map/ppermute | solution.py:158
  8.5 2.6 %collective-permute-start.87 = (bf16[16,2176]{1,0:T(8,128)(2,1)S(1)}, bf16[16,2176]{1,0:T(8,128)(2,1)S(1)}, u32[]{:S(2)}, u32[]{:S(2)}) collective-permute-start(bf16[16,2176]{1,0:T(8,128)(2,1)S(1)} %pad_maximum_fusion.1.refs_0_), channel_id=1, source_target_pairs={{0,4},{1,5},{2,6},{3,7},{4,0},{5,1},{6,2},{7,3},{8,12},{9,13},{10,... | collective-permute-start | bytes 208904 | tf_op jit(solution)/shard_map/ppermute | solution.py:158
  11.1 1.7 %collective-permute-start.89 = (bf16[16,2176]{1,0:T(8,128)(2,1)S(1)}, bf16[16,2176]{1,0:T(8,128)(2,1)S(1)}, u32[]{:S(2)}, u32[]{:S(2)}) collective-permute-start(bf16[16,2176]{1,0:T(8,128)(2,1)S(1)} %pad_maximum_fusion.1.refs_0_), channel_id=1, source_target_pairs={{0,8},{8,0},{16,24},{24,16},{1,9},{9,1},{17,25},{25,17},{2,10},{10... | collective-permute-start | bytes 208904 | tf_op jit(solution)/shard_map/ppermute | solution.py:158
  12.8 1.5 %collective-permute-start.90 = (bf16[16,2176]{1,0:T(8,128)(2,1)S(1)}, bf16[16,2176]{1,0:T(8,128)(2,1)S(1)}, u32[]{:S(2)}, u32[]{:S(2)}) collective-permute-start(bf16[16,2176]{1,0:T(8,128)(2,1)S(1)} %pad_maximum_fusion.1.refs_0_), channel_id=1, source_target_pairs={{0,16},{8,24},{16,0},{24,8},{1,17},{9,25},{17,1},{25,9},{2,18},{10... | collective-permute-start | bytes 208904 | tf_op jit(solution)/shard_map/ppermute | solution.py:158
  14.3 1.0 %slice_bitcast_fusion.2 = (bf16[64,1024]{1,0:T(8,128)(2,1)S(1)}, bf16[64,1024]{1,0:T(8,128)(2,1)S(1)}) fusion(bf16[1,1,384,1024]{3,2,1,0:T(8,128)(2,1)} %param.26), kind=kLoop, calls=%fused_computation.4 | loop fusion | bytes 524288 | tf_op jit(solution)/shard_map/squeeze | solution.py:320
  15.3 0.9 %slice_bitcast_fusion = bf16[64,1024]{1,0:T(8,128)(2,1)S(1)} fusion(bf16[1,1,192,1024]{3,2,1,0:T(8,128)(2,1)} %param.27), kind=kLoop, calls=%fused_computation.2 | loop fusion | bytes 262144 | tf_op jit(solution)/shard_map/squeeze | solution.py:320
  16.2 0.3 collective-permute-start.91
  16.6 0.7 collective-permute-done.88.refs_6_
  17.3 0.6 copy-done.3
  18.0 3.6 %collective-permute-done.91.refs_3_ = bf16[16,2176]{1,0:T(8,128)(2,1)S(1)} collective-permute-done((bf16[16,2176]{1,0:T(8,128)(2,1)S(1)}, bf16[16,2176]{1,0:T(8,128)(2,1)S(1)}, u32[]{:S(2)}, u32[]{:S(2)}) %collective-permute-start.91) | collective-permute-done | bytes 69664 | tf_op jit(solution)/shard_map/ppermute | solution.py:158
  21.5 0.6 copy-done.5
  22.1 0.6 constant_dynamic-update-slice_fusion.2
  22.8 1.7 %collective-permute-start.95 = (bf16[192,1024]{1,0:T(8,128)(2,1)S(1)}, bf16[192,1024]{1,0:T(8,128)(2,1)S(1)}, u32[]{:S(2)}, u32[]{:S(2)}) collective-permute-start(bf16[192,1024]{1,0:T(8,128)(2,1)S(1)} %pad_maximum_fusion.early_own), channel_id=1, source_target_pairs={{0,4},{1,5},{2,6},{3,7},{4,0},{5,1},{6,2},{7,3},{8,12},{9,13},{10,... | collective-permute-start | bytes 1179656 | tf_op jit(solution)/shard_map/ppermute | solution.py:158
  24.5 0.6 constant_dynamic-update-slice_fusion.1
  25.1 0.6 constant_dynamic-update-slice_fusion
  25.7 0.5 collective-permute-start.92
  26.3 0.5 collective-permute-start.93
  26.8 2.4 %collective-permute-start.94 = (bf16[48,2176]{1,0:T(8,128)(2,1)}, bf16[48,2176]{1,0:T(8,128)(2,1)}, u32[]{:S(2)}, u32[]{:S(2)}) collective-permute-start(bf16[48,2176]{1,0:T(8,128)(2,1)} %constant_dynamic-update-slice_fusion), channel_id=1, source_target_pairs={{0,24},{8,16},{16,8},{24,0},{1,25},{9,17},{17,9},{25,1},{2,26},{10... | collective-permute-start | bytes 626696 | tf_op jit(solution)/shard_map/ppermute | solution.py:158
  29.9 2.7 %collective-permute-done.92.refs_7_ = bf16[48,2176]{1,0:T(8,128)(2,1)} collective-permute-done((bf16[48,2176]{1,0:T(8,128)(2,1)}, bf16[48,2176]{1,0:T(8,128)(2,1)}, u32[]{:S(2)}, u32[]{:S(2)}) %collective-permute-start.92) | collective-permute-done | bytes 208928 | tf_op jit(solution)/shard_map/ppermute | solution.py:158
  32.6 2.5 %collective-permute-done.93.refs_8_ = bf16[48,2176]{1,0:T(8,128)(2,1)} collective-permute-done((bf16[48,2176]{1,0:T(8,128)(2,1)}, bf16[48,2176]{1,0:T(8,128)(2,1)}, u32[]{:S(2)}, u32[]{:S(2)}) %collective-permute-start.93) | collective-permute-done | bytes 208928 | tf_op jit(solution)/shard_map/ppermute | solution.py:158
  35.1 0.9 %copy-done.4 = bf16[16,2176]{1,0:T(8,128)(2,1)S(1)} copy-done((bf16[16,2176]{1,0:T(8,128)(2,1)S(1)}, bf16[16,2176]{1,0:T(8,128)(2,1)}, u32[]{:S(2)}) %copy-start.4) | copy-done | bytes 69656
  36.0 0.9 %copy-done.6 = bf16[16,2176]{1,0:T(8,128)(2,1)S(1)} copy-done((bf16[16,2176]{1,0:T(8,128)(2,1)S(1)}, bf16[16,2176]{1,0:T(8,128)(2,1)}, u32[]{:S(2)}) %copy-start.6) | copy-done | bytes 69656
  36.9 3.9 %forward.1 = (bf16[256,2176]{1,0:T(8,128)(2,1)S(1)}, bf16[384,256]{1,0:T(8,128)(2,1)S(1)}, bf16[384,256]{1,0:T(8,128)(2,1)S(1)}, f32[4,16,1024]{2,1,0:T(8,128)S(...) custom-call(bf16[16,2176]{1,0:T(8,128)(2,1)S(1)} %pad_maximum_fusion.1.refs, ...), custom_call_target="tpu_custom_call" | custom-call | tf_op jit(solution)/shard_map/forward/pallas_call | solution.py:331
  40.8 0.7 copy-done.2
  41.5 1.0 %copy-done.7 = bf16[256,2176]{1,0:T(8,128)(2,1)} copy-done((bf16[256,2176]{1,0:T(8,128)(2,1)}, bf16[256,2176]{1,0:T(8,128)(2,1)S(1)}, u32[]{:S(2)}) %copy-start.7) | copy-done | bytes 1114136
  42.5 17.5 %conditional.1 = (bf16[384,256]{1,0:T(8,128)(2,1)}, bf16[384,256]{1,0:T(8,128)(2,1)}, bf16[256,2176]{1,0:T(8,128)(2,1)}, bf16[4,16,1024]{2,1,0:T(8,128)(2,1)}, b...) conditional(s32[]{:T(128)} %clamp.3, (bf16[384,256]{1,0:T(8,128)(2,1)S(1)}, ...), branch_computations={%region_1.2_spmd, %region_2.3_spmd, %region_3.4_spmd, %region_4.5_... | conditional | bytes 7602464 | solution.py:349
  42.5 3.2 %collective-permute-start = (bf16[384,256]{1,0:T(8,128)(2,1)S(1)}, bf16[384,256]{1,0:T(8,128)(2,1)}, u32[]{:S(2)}, u32[]{:S(2)}) collective-permute-start(bf16[384,256]{1,0:T(8,128)(2,1)S(1)} %get-tuple-element.168), channel_id=1, source_target_pairs={{0,4},{1,1},{2,2},{3,3},{4,0},{5,5},{6,6},{7,7},{8,12},{9,9},{10,1... | collective-permute-start | bytes 589832 | tf_op jit(solution)/shard_map/cond/branch_0_fun/ppermute | solution.py:293
  45.7 1.6 %collective-permute-start.1 = (bf16[4,16,1024]{2,1,0:T(8,128)(2,1)S(1)}, bf16[4,16,1024]{2,1,0:T(8,128)(2,1)}, u32[]{:S(2)}, u32[]{:S(2)}) collective-permute-start(bf16[4,16,1024]{2,1,0:T(8,128)(2,1)S(1)} %get-tuple-element.171), channel_id=1, source_target_pairs={{0,8},{8,0},{16,24},{24,16},{1,9},{9,1},{17,25},{25,17},{2,10},{10... | collective-permute-start | bytes 393224 | tf_op jit(solution)/shard_map/cond/branch_0_fun/ppermute | solution.py:158
  47.3 0.7 collective-permute-start.2
  48.0 1.3 %collective-permute-start.3 = (bf16[4,16,1024]{2,1,0:T(8,128)(2,1)S(1)}, bf16[4,16,1024]{2,1,0:T(8,128)(2,1)}, u32[]{:S(2)}, u32[]{:S(2)}) collective-permute-start(bf16[4,16,1024]{2,1,0:T(8,128)(2,1)S(1)} %get-tuple-element.173), channel_id=1, source_target_pairs={{0,24},{8,16},{16,8},{24,0},{1,25},{9,17},{17,9},{25,1},{2,26},{10... | collective-permute-start | bytes 393224 | tf_op jit(solution)/shard_map/cond/branch_0_fun/ppermute | solution.py:158
  49.3 1.8 %collective-permute-done = bf16[384,256]{1,0:T(8,128)(2,1)} collective-permute-done((bf16[384,256]{1,0:T(8,128)(2,1)S(1)}, bf16[384,256]{1,0:T(8,128)(2,1)}, u32[]{:S(2)}, u32[]{:S(2)}) %collective-permute-start) | collective-permute-done | bytes 196640 | tf_op jit(solution)/shard_map/cond/branch_0_fun/ppermute | solution.py:293
  51.1 1.3 %collective-permute-done.2 = bf16[4,16,1024]{2,1,0:T(8,128)(2,1)} collective-permute-done((bf16[4,16,1024]{2,1,0:T(8,128)(2,1)S(1)}, bf16[4,16,1024]{2,1,0:T(8,128)(2,1)}, u32[]{:S(2)}, u32[]{:S(2)}) %collective-permute-start.2) | collective-permute-done | bytes 131104 | tf_op jit(solution)/shard_map/cond/branch_0_fun/ppermute | solution.py:158
  52.4 1.6 %collective-permute-done.3 = bf16[4,16,1024]{2,1,0:T(8,128)(2,1)} collective-permute-done((bf16[4,16,1024]{2,1,0:T(8,128)(2,1)S(1)}, bf16[4,16,1024]{2,1,0:T(8,128)(2,1)}, u32[]{:S(2)}, u32[]{:S(2)}) %collective-permute-start.3) | collective-permute-done | bytes 131104 | tf_op jit(solution)/shard_map/cond/branch_0_fun/ppermute | solution.py:158
  54.0 0.5 collective-permute-start.4
  54.5 5.6 %collective-permute-done.4 = bf16[384,256]{1,0:T(8,128)(2,1)} collective-permute-done((bf16[384,256]{1,0:T(8,128)(2,1)S(1)}, bf16[384,256]{1,0:T(8,128)(2,1)}, u32[]{:S(2)}, u32[]{:S(2)}) %collective-permute-start.4) | collective-permute-done | bytes 196640 | tf_op jit(solution)/shard_map/cond/branch_0_fun/ppermute | solution.py:296
  60.1 1.3 %fusion.7 = (bf16[4,16,1024]{2,1,0:T(8,128)(2,1)S(1)}, f32[4,16,1024]{2,1,0:T(8,128)S(1)}) fusion(bf16[4,16,1024]{2,1,0:T(8,128)(2,1)} %get-tuple-element.410, bf16[4,16,1024]{2,1,0:T(8,128)(2,1)} %get-tuple-element.409, f32[4,16,1024]{2,1,0:T(8,128)} %copy-done.2, bf16[4,16,1024]{2,1,0:T(8,128)(2,1)} %get-tuple-element.408), kind=kLoop, calls=%fused_computation.49 | loop fusion | flops 458752 | bytes 1048576 | tf_op jit(solution)/shard_map/convert_element_type | solution.py:354
  61.5 1.7 %collective-permute-start.97 = (bf16[16,1024]{1,0:T(8,128)(2,1)S(1)}, bf16[16,1024]{1,0:T(8,128)(2,1)S(1)}, u32[]{:S(2)}, u32[]{:S(2)}) collective-permute-start(bf16[16,1024]{1,0:T(8,128)(2,1)S(1)} %get-tuple-element.423), channel_id=1, source_target_pairs={{0,4},{1,5},{2,6},{3,7},{4,0},{5,1},{6,2},{7,3},{8,12},{9,13},{10,... | collective-permute-start | bytes 98312 | tf_op jit(solution)/shard_map/ppermute | solution.py:158
  63.2 2.7 %collective-permute-start.98 = (bf16[16,1024]{1,0:T(8,128)(2,1)S(1)}, bf16[16,1024]{1,0:T(8,128)(2,1)S(1)}, u32[]{:S(2)}, u32[]{:S(2)}) collective-permute-start(bf16[16,1024]{1,0:T(8,128)(2,1)S(1)} %get-tuple-element.422), channel_id=1, source_target_pairs={{0,6},{1,7},{2,4},{3,5},{4,2},{5,3},{6,0},{7,1},{8,14},{9,15},{10,... | collective-permute-start | bytes 98312 | tf_op jit(solution)/shard_map/ppermute | solution.py:158
  65.8 0.1 copy.10.relocate_ref
  65.9 4.3 %weight_grads.1 = (bf16[384,1024]{1,0:T(8,128)(2,1)}, bf16[192,1024]{1,0:T(8,128)(2,1)}) custom-call(s32[8,1]{1,0:T(8,128)S(1)} %copy.10.relocate_ref, bf16[384,256]{1,0:T(8,128)(2,1)} %get-tuple-element.411.same_ref, bf16[384,256]{1,0:T(8,128)(2,1)} %get-tuple-element.412.cross_ref, bf16[192,1024]{1,0:T(8,128)(2,1)S(1)} %pad_maximum_fusion.early_own, ...), custom_call_target="tpu_custom_call" | custom-call | tf_op jit(solution)/shard_map/weight_grads/pallas_call | solution.py:358
  70.2 0.6 fusion.3
  (35 shorter events, 0.2 us)
Async XLA Ops:
  0.6 34.5 %copy-start = (bf16[1,1,384,1024]{3,2,1,0:T(8,128)(2,1)S(1)}, bf16[1,1,384,1024]{3,2,1,0:T(8,128)(2,1)}, u32[]{:S(2)}) copy-start(bf16[1,1,384,1024]{3,2,1,0:T(8,128)(2,1)} %param.26) | copy-start | bytes 2359300
  0.6 34.5 %copy-start.1 = (bf16[1,1,192,1024]{3,2,1,0:T(8,128)(2,1)S(1)}, bf16[1,1,192,1024]{3,2,1,0:T(8,128)(2,1)}, u32[]{:S(2)}) copy-start(bf16[1,1,192,1024]{3,2,1,0:T(8,128)(2,1)} %param.27) | copy-start | bytes 1179652
  0.7 4.8 %collective-permute-start.84 = (bf16[384,1024]{1,0:T(8,128)(2,1)}, bf16[384,1024]{1,0:T(8,128)(2,1)S(1)}, u32[]{:S(2)}, u32[]{:S(2)}) collective-permute-start(bf16[384,1024]{1,0:T(8,128)(2,1)} %bitcast.62), channel_id=1, source_target_pairs={{0,1},{1,0},{2,3},{3,2},{4,5},{5,4},{6,7},{7,6},{8,9},{9,8},{10,11... | collective-permute-start | bytes 2359304 | tf_op jit(solution)/shard_map/ppermute | solution.py:158
  1.2 4.3 %collective-permute-start.85 = (bf16[192,1024]{1,0:T(8,128)(2,1)}, bf16[192,1024]{1,0:T(8,128)(2,1)S(1)}, u32[]{:S(2)}, u32[]{:S(2)}) collective-permute-start(bf16[192,1024]{1,0:T(8,128)(2,1)} %bitcast.64), channel_id=1, source_target_pairs={{0,1},{1,0},{2,3},{3,2},{4,5},{5,4},{6,7},{7,6},{8,9},{9,8},{10,11... | collective-permute-start | bytes 1179656 | tf_op jit(solution)/shard_map/ppermute | solution.py:158
  5.4 10.8 %collective-permute-start.86 = (bf16[16,2176]{1,0:T(8,128)(2,1)S(1)}, bf16[16,2176]{1,0:T(8,128)(2,1)S(1)}, u32[]{:S(2)}, u32[]{:S(2)}) collective-permute-start(bf16[16,2176]{1,0:T(8,128)(2,1)S(1)} %pad_maximum_fusion.1.refs_0_), channel_id=1, source_target_pairs={{0,2},{1,3},{2,0},{3,1},{4,6},{5,7},{6,4},{7,5},{8,10},{9,11},{10,... | collective-permute-start | bytes 208904 | tf_op jit(solution)/shard_map/ppermute | solution.py:158
  8.5 8.1 %collective-permute-start.87 = (bf16[16,2176]{1,0:T(8,128)(2,1)S(1)}, bf16[16,2176]{1,0:T(8,128)(2,1)S(1)}, u32[]{:S(2)}, u32[]{:S(2)}) collective-permute-start(bf16[16,2176]{1,0:T(8,128)(2,1)S(1)} %pad_maximum_fusion.1.refs_0_), channel_id=1, source_target_pairs={{0,4},{1,5},{2,6},{3,7},{4,0},{5,1},{6,2},{7,3},{8,12},{9,13},{10,... | collective-permute-start | bytes 208904 | tf_op jit(solution)/shard_map/ppermute | solution.py:158
  11.1 6.2 %collective-permute-start.88 = (bf16[16,2176]{1,0:T(8,128)(2,1)S(1)}, bf16[16,2176]{1,0:T(8,128)(2,1)S(1)}, u32[]{:S(2)}, u32[]{:S(2)}) collective-permute-start(bf16[16,2176]{1,0:T(8,128)(2,1)S(1)} %pad_maximum_fusion.1.refs_0_), channel_id=1, source_target_pairs={{0,6},{1,7},{2,4},{3,5},{4,2},{5,3},{6,0},{7,1},{8,14},{9,15},{10,... | collective-permute-start | bytes 208904 | tf_op jit(solution)/shard_map/ppermute | solution.py:158
  11.1 6.2 %collective-permute-start.89 = (bf16[16,2176]{1,0:T(8,128)(2,1)S(1)}, bf16[16,2176]{1,0:T(8,128)(2,1)S(1)}, u32[]{:S(2)}, u32[]{:S(2)}) collective-permute-start(bf16[16,2176]{1,0:T(8,128)(2,1)S(1)} %pad_maximum_fusion.1.refs_0_), channel_id=1, source_target_pairs={{0,8},{8,0},{16,24},{24,16},{1,9},{9,1},{17,25},{25,17},{2,10},{10... | collective-permute-start | bytes 208904 | tf_op jit(solution)/shard_map/ppermute | solution.py:158
  12.8 4.5 %collective-permute-start.90 = (bf16[16,2176]{1,0:T(8,128)(2,1)S(1)}, bf16[16,2176]{1,0:T(8,128)(2,1)S(1)}, u32[]{:S(2)}, u32[]{:S(2)}) collective-permute-start(bf16[16,2176]{1,0:T(8,128)(2,1)S(1)} %pad_maximum_fusion.1.refs_0_), channel_id=1, source_target_pairs={{0,16},{8,24},{16,0},{24,8},{1,17},{9,25},{17,1},{25,9},{2,18},{10... | collective-permute-start | bytes 208904 | tf_op jit(solution)/shard_map/ppermute | solution.py:158
  16.2 5.3 %collective-permute-start.91 = (bf16[16,2176]{1,0:T(8,128)(2,1)S(1)}, bf16[16,2176]{1,0:T(8,128)(2,1)S(1)}, u32[]{:S(2)}, u32[]{:S(2)}) collective-permute-start(bf16[16,2176]{1,0:T(8,128)(2,1)S(1)} %pad_maximum_fusion.1.refs_0_), channel_id=1, source_target_pairs={{0,24},{8,16},{16,8},{24,0},{1,25},{9,17},{17,9},{25,1},{2,26},{10... | collective-permute-start | bytes 208904 | tf_op jit(solution)/shard_map/ppermute | solution.py:158
  17.3 0.6 copy-start.3
  21.5 0.6 copy-start.5
  22.8 37.3 %collective-permute-start.95 = (bf16[192,1024]{1,0:T(8,128)(2,1)S(1)}, bf16[192,1024]{1,0:T(8,128)(2,1)S(1)}, u32[]{:S(2)}, u32[]{:S(2)}) collective-permute-start(bf16[192,1024]{1,0:T(8,128)(2,1)S(1)} %pad_maximum_fusion.early_own), channel_id=1, source_target_pairs={{0,4},{1,5},{2,6},{3,7},{4,0},{5,1},{6,2},{7,3},{8,12},{9,13},{10,... | collective-permute-start | bytes 1179656 | tf_op jit(solution)/shard_map/ppermute | solution.py:158
  25.7 6.9 %collective-permute-start.92 = (bf16[48,2176]{1,0:T(8,128)(2,1)}, bf16[48,2176]{1,0:T(8,128)(2,1)}, u32[]{:S(2)}, u32[]{:S(2)}) collective-permute-start(bf16[48,2176]{1,0:T(8,128)(2,1)} %constant_dynamic-update-slice_fusion), channel_id=1, source_target_pairs={{0,8},{8,0},{16,24},{24,16},{1,9},{9,1},{17,25},{25,17},{2,10},{10... | collective-permute-start | bytes 626696 | tf_op jit(solution)/shard_map/ppermute | solution.py:158
  26.3 8.8 %collective-permute-start.93 = (bf16[48,2176]{1,0:T(8,128)(2,1)}, bf16[48,2176]{1,0:T(8,128)(2,1)}, u32[]{:S(2)}, u32[]{:S(2)}) collective-permute-start(bf16[48,2176]{1,0:T(8,128)(2,1)} %constant_dynamic-update-slice_fusion), channel_id=1, source_target_pairs={{0,16},{8,24},{16,0},{24,8},{1,17},{9,25},{17,1},{25,9},{2,18},{10... | collective-permute-start | bytes 626696 | tf_op jit(solution)/shard_map/ppermute | solution.py:158
  26.8 8.3 %collective-permute-start.94 = (bf16[48,2176]{1,0:T(8,128)(2,1)}, bf16[48,2176]{1,0:T(8,128)(2,1)}, u32[]{:S(2)}, u32[]{:S(2)}) collective-permute-start(bf16[48,2176]{1,0:T(8,128)(2,1)} %constant_dynamic-update-slice_fusion), channel_id=1, source_target_pairs={{0,24},{8,16},{16,8},{24,0},{1,25},{9,17},{17,9},{25,1},{2,26},{10... | collective-permute-start | bytes 626696 | tf_op jit(solution)/shard_map/ppermute | solution.py:158
  35.1 0.9 %copy-start.4 = (bf16[16,2176]{1,0:T(8,128)(2,1)S(1)}, bf16[16,2176]{1,0:T(8,128)(2,1)}, u32[]{:S(2)}) copy-start(bf16[16,2176]{1,0:T(8,128)(2,1)} %copy-done.3) | copy-start | bytes 208900
  36.0 0.9 %copy-start.6 = (bf16[16,2176]{1,0:T(8,128)(2,1)S(1)}, bf16[16,2176]{1,0:T(8,128)(2,1)}, u32[]{:S(2)}) copy-start(bf16[16,2176]{1,0:T(8,128)(2,1)} %copy-done.5) | copy-start | bytes 208900
  40.8 0.7 copy-start.2
  41.5 1.0 %copy-start.7 = (bf16[256,2176]{1,0:T(8,128)(2,1)}, bf16[256,2176]{1,0:T(8,128)(2,1)S(1)}, u32[]{:S(2)}) copy-start(bf16[256,2176]{1,0:T(8,128)(2,1)S(1)} %get-tuple-element.403.plane_ref) | copy-start | bytes 3342340
  41.5 24.3 %copy-start.9 = (s32[8,1]{0,1:T(1,128)S(1)}, s32[8,1]{0,1:T(1,128)}, u32[]{:S(2)}) copy-start(s32[8,1]{0,1:T(1,128)} %param.25) | copy-start | bytes 100
  42.5 8.6 %collective-permute-start = (bf16[384,256]{1,0:T(8,128)(2,1)S(1)}, bf16[384,256]{1,0:T(8,128)(2,1)}, u32[]{:S(2)}, u32[]{:S(2)}) collective-permute-start(bf16[384,256]{1,0:T(8,128)(2,1)S(1)} %get-tuple-element.168), channel_id=1, source_target_pairs={{0,4},{1,1},{2,2},{3,3},{4,0},{5,5},{6,6},{7,7},{8,12},{9,9},{10,1... | collective-permute-start | bytes 589832 | tf_op jit(solution)/shard_map/cond/branch_0_fun/ppermute | solution.py:293
  45.7 5.4 %collective-permute-start.1 = (bf16[4,16,1024]{2,1,0:T(8,128)(2,1)S(1)}, bf16[4,16,1024]{2,1,0:T(8,128)(2,1)}, u32[]{:S(2)}, u32[]{:S(2)}) collective-permute-start(bf16[4,16,1024]{2,1,0:T(8,128)(2,1)S(1)} %get-tuple-element.171), channel_id=1, source_target_pairs={{0,8},{8,0},{16,24},{24,16},{1,9},{9,1},{17,25},{25,17},{2,10},{10... | collective-permute-start | bytes 393224 | tf_op jit(solution)/shard_map/cond/branch_0_fun/ppermute | solution.py:158
  47.3 5.1 %collective-permute-start.2 = (bf16[4,16,1024]{2,1,0:T(8,128)(2,1)S(1)}, bf16[4,16,1024]{2,1,0:T(8,128)(2,1)}, u32[]{:S(2)}, u32[]{:S(2)}) collective-permute-start(bf16[4,16,1024]{2,1,0:T(8,128)(2,1)S(1)} %get-tuple-element.172), channel_id=1, source_target_pairs={{0,16},{8,24},{16,0},{24,8},{1,17},{9,25},{17,1},{25,9},{2,18},{10... | collective-permute-start | bytes 393224 | tf_op jit(solution)/shard_map/cond/branch_0_fun/ppermute | solution.py:158
  48.0 6.0 %collective-permute-start.3 = (bf16[4,16,1024]{2,1,0:T(8,128)(2,1)S(1)}, bf16[4,16,1024]{2,1,0:T(8,128)(2,1)}, u32[]{:S(2)}, u32[]{:S(2)}) collective-permute-start(bf16[4,16,1024]{2,1,0:T(8,128)(2,1)S(1)} %get-tuple-element.173), channel_id=1, source_target_pairs={{0,24},{8,16},{16,8},{24,0},{1,25},{9,17},{17,9},{25,1},{2,26},{10... | collective-permute-start | bytes 393224 | tf_op jit(solution)/shard_map/cond/branch_0_fun/ppermute | solution.py:158
  54.0 6.1 %collective-permute-start.5 = (bf16[256,2176]{1,0:T(8,128)(2,1)S(1)}, bf16[256,2176]{1,0:T(8,128)(2,1)}, u32[]{:S(2)}, u32[]{:S(2)}) collective-permute-start(bf16[256,2176]{1,0:T(8,128)(2,1)S(1)} %get-tuple-element.177), channel_id=1, source_target_pairs={{0,1},{1,0},{2,3},{3,2},{4,5},{5,4},{6,7},{7,6},{8,9},{9,8},{10,11... | collective-permute-start | bytes 3342344 | tf_op jit(solution)/shard_map/cond/branch_0_fun/ppermute | solution.py:158
  54.0 6.1 %collective-permute-start.4 = (bf16[384,256]{1,0:T(8,128)(2,1)S(1)}, bf16[384,256]{1,0:T(8,128)(2,1)}, u32[]{:S(2)}, u32[]{:S(2)}) collective-permute-start(bf16[384,256]{1,0:T(8,128)(2,1)S(1)} %get-tuple-element.176), channel_id=1, source_target_pairs={{0,1},{1,4},{2,3},{3,2},{4,5},{5,0},{6,7},{7,6},{8,9},{9,12},{10,1... | collective-permute-start | bytes 589832 | tf_op jit(solution)/shard_map/cond/branch_0_fun/ppermute | solution.py:296
  60.1 5.8 %copy-start.8 = (bf16[256,2176]{1,0:T(8,128)(2,1)S(1)}, bf16[256,2176]{1,0:T(8,128)(2,1)}, u32[]{:S(2)}) copy-start(bf16[256,2176]{1,0:T(8,128)(2,1)} %copy-done.7) | copy-start | bytes 3342340
  61.4 8.8 %collective-permute-start.96 = (bf16[16,1024]{1,0:T(8,128)(2,1)S(1)}, bf16[16,1024]{1,0:T(8,128)(2,1)S(1)}, u32[]{:S(2)}, u32[]{:S(2)}) collective-permute-start(bf16[16,1024]{1,0:T(8,128)(2,1)S(1)} %get-tuple-element.421), channel_id=1, source_target_pairs={{0,2},{1,3},{2,0},{3,1},{4,6},{5,7},{6,4},{7,5},{8,10},{9,11},{10,... | collective-permute-start | bytes 98312 | tf_op jit(solution)/shard_map/ppermute | solution.py:158
  61.5 8.7 %collective-permute-start.97 = (bf16[16,1024]{1,0:T(8,128)(2,1)S(1)}, bf16[16,1024]{1,0:T(8,128)(2,1)S(1)}, u32[]{:S(2)}, u32[]{:S(2)}) collective-permute-start(bf16[16,1024]{1,0:T(8,128)(2,1)S(1)} %get-tuple-element.423), channel_id=1, source_target_pairs={{0,4},{1,5},{2,6},{3,7},{4,0},{5,1},{6,2},{7,3},{8,12},{9,13},{10,... | collective-permute-start | bytes 98312 | tf_op jit(solution)/shard_map/ppermute | solution.py:158
  63.2 7.0 %collective-permute-start.98 = (bf16[16,1024]{1,0:T(8,128)(2,1)S(1)}, bf16[16,1024]{1,0:T(8,128)(2,1)S(1)}, u32[]{:S(2)}, u32[]{:S(2)}) collective-permute-start(bf16[16,1024]{1,0:T(8,128)(2,1)S(1)} %get-tuple-element.422), channel_id=1, source_target_pairs={{0,6},{1,7},{2,4},{3,5},{4,2},{5,3},{6,0},{7,1},{8,14},{9,15},{10,... | collective-permute-start | bytes 98312 | tf_op jit(solution)/shard_map/ppermute | solution.py:158
